TPU v7x, 256 devices: a whole 4x4x8 slice. The times are simulated.
256 devices in a mesh: sub: 64 (over z, y, core), inner: 4 (over x).
Axes of the slice: x: 4, y: 4, z: 8, core: 2. Of those that a mesh axis runs over, the one named last changes fastest.
Arguments:
- solution: float32 [32, 3, 256, 16, 128], P(None, None, 'sub', 'inner'), may hold values from -6 to 6
- residual: float32 [32, 3, 256, 16, 128], P(None, None, 'sub', 'inner'), may hold values from -6 to 6
- direction: float32 [32, 3, 256, 16, 128], P(None, None, 'sub', 'inner'), may hold values from -6 to 6
- mass: float32 [256, 16, 128], P('sub', 'inner'), may hold values from 0.2 to 5
- coarse_basis: float32 [32, 3, 256, 16, 128], P(None, None, 'sub', 'inner'), may hold values from -1 to 1
- line_inverse: float32 [64, 4, 128, 128], P('sub', 'inner'), may hold values from -1.5 to 1.5
- coarse_factor: float32 [8192, 8192], P(('sub', 'inner')), may hold values from -1 to 1
Outputs:
- new_solution: float32 [32, 3, 256, 16, 128], P(None, None, 'sub', 'inner')
- new_residual: float32 [32, 3, 256, 16, 128], P(None, None, 'sub', 'inner')
- new_direction: float32 [32, 3, 256, 16, 128], P(None, None, 'sub', 'inner')
All inputs are finite; a program needn't handle non-finite values.
Results may differ from a plain program's by a relative error of at most 0.00017.
Values sent between devices are 32-bit elements; how exact they have to be, the bound alone decides.
No kernel may reach another device: no remote copies, remote signals or barrier semaphores. Data moves between devices by JAX's collectives and lax.ppermute only.
A program may use at most 64 MiB of HBM per device.

v0:
```python
import jax
import jax.numpy as jnp
from jax import lax
from jax.experimental import pallas as pl
from jax.experimental.pallas import tpu as pltpu
from jax.sharding import Mesh
from jax.sharding import PartitionSpec as P

SUB = ("z", "y", "core")
ROWS = ("y", "x")
COLS = ("z", "core")
exact = lax.Precision.HIGHEST

K = 32
F = 48
LANES = 128


def dot(a, b, dims=((1,), (0,))):
    return lax.dot_general(a, b, (dims, ((), ())), precision=exact, preferred_element_type=jnp.float32)


def line(ref, f):
    return ref[pl.ds(f, K, stride=F), :]


def place(c, x, y):
    return (c * 4 + x) * 4 + y


def wide(ref):
    return jnp.concatenate([line(ref, f) for f in range(F)], axis=1)


def narrow(value, ref):
    for f in range(F):
        ref[pl.ds(f, K, stride=F), :] = value[:, f * LANES : (f + 1) * LANES]


def call(kernel, outs, scratch=(), flops=10_000_000, name=None):
    vmem = pl.BlockSpec(memory_space=pltpu.VMEM)

    def run(*args):
        moved = 4 * (sum(a.size for a in args) + sum(o[0] * o[1] if len(o) == 2 else o[0] * o[1] * o[2] for o in outs))
        return pl.pallas_call(
            kernel,
            out_shape=[jax.ShapeDtypeStruct(o, jnp.float32) for o in outs],
            in_specs=[vmem] * len(args),
            out_specs=[vmem] * len(outs),
            scratch_shapes=list(scratch),
            compiler_params=pltpu.CompilerParams(vmem_limit_bytes=40 * 1024 * 1024),
            cost_estimate=pl.CostEstimate(flops=flops, bytes_accessed=moved, transcendentals=0),
            name=name,
        )(*args)

    return run


def slab_kernel(p, low_x, high_x, low_y, high_y):
    at = 0
    for c in range(3):
        for x in range(2):
            for y in range(4):
                low_x[pl.ds(at * K, K), :] = line(p, place(c, x, y))
                high_x[pl.ds(at * K, K), :] = line(p, place(c, x + 2, y))
                at += 1
    at = 0
    for c in range(3):
        for x in range(4):
            for y in range(2):
                low_y[pl.ds(at * K, K), :] = line(p, place(c, x, y))
                high_y[pl.ds(at * K, K), :] = line(p, place(c, x, y + 2))
                at += 1


def lined_kernel(r, inverse, lined_r):
    lined_r[...] = dot(r[...], inverse[...], ((1,), (1,)))


def image_kernel(p, r, basis, mass, below_x, above_x, below_y, above_y, q, sums, left, right):
    lane = lax.broadcasted_iota(jnp.int32, (K, LANES), 1)

    def at(c, x, y):
        if x < 0:
            return below_x[pl.ds(((c * 2 + x + 2) * 4 + y) * K, K), :]
        if x > 3:
            return above_x[pl.ds(((c * 2 + x - 4) * 4 + y) * K, K), :]
        if y < 0:
            return below_y[pl.ds(((c * 4 + x) * 2 + y + 2) * K, K), :]
        if y > 3:
            return above_y[pl.ds(((c * 4 + x) * 2 + y - 4) * K, K), :]
        return left[pl.ds(0, K), pl.ds(place(c, x, y) * LANES, LANES)]

    for f in range(F):
        columns = pl.ds(f * LANES, LANES)
        left[pl.ds(0, K), columns] = line(p, f)
        left[pl.ds(K, K), columns] = line(basis, f)
        right[pl.ds(K, K), columns] = line(r, f)
    for c in range(3):
        for x in range(4):
            for y in range(4):
                f = place(c, x, y)
                center = at(c, x, y)
                near = at(c, x - 1, y) + at(c, x + 1, y) + at(c, x, y - 1) + at(c, x, y + 1)
                far = at(c, x - 2, y) + at(c, x + 2, y) + at(c, x, y - 2) + at(c, x, y + 2)
                near = near + jnp.where(lane >= 1, pltpu.roll(center, 1, 1), 0.0)
                near = near + jnp.where(lane < LANES - 1, pltpu.roll(center, LANES - 1, 1), 0.0)
                far = far + jnp.where(lane >= 2, pltpu.roll(center, 2, 1), 0.0)
                far = far + jnp.where(lane < LANES - 2, pltpu.roll(center, LANES - 2, 1), 0.0)
                weight = mass[pl.ds(x * 4 + y, 1), :] + 7.5
                value = weight * center - (4.0 / 3.0) * near + (1.0 / 12.0) * far
                right[pl.ds(0, K), pl.ds(f * LANES, LANES)] = value
                q[:, pl.ds(f * LANES, LANES)] = value
    both = dot(left[...], right[...], ((1,), (1,)))
    packed = jnp.concatenate([both[:K], both[K:]], axis=1)
    for g in range(16):
        sums[g] = packed


def image_lined_kernel(q, lined_r, inverse, lined_q, inner, right):
    for f in range(F):
        columns = pl.ds(f * LANES, LANES)
        right[pl.ds(f * K, K), :] = q[:, columns]
    right[...] = dot(right[...], inverse[...], ((1,), (1,)))
    for f in range(F):
        columns = pl.ds(f * LANES, LANES)
        lined_q[pl.ds(0, K), columns] = right[pl.ds(f * K, K), :]
        lined_q[pl.ds(K, K), columns] = line(lined_r, f)
    inner[...] = dot(q[...], lined_q[...], ((1,), (1,)))


def mid_kernel(gathered, factor, out):
    total = jnp.sum(gathered[...], axis=0)
    rhs = jnp.concatenate([gathered[g][:, 64:] for g in range(16)], axis=0)
    mid = dot(rhs.T, factor[...].reshape(512, 512)).T
    for g in range(16):
        out[g] = jnp.concatenate([mid[g * K : (g + 1) * K], total[:, :64]], axis=1)


def packed4(a, b):
    return jnp.concatenate([a[:16], a[16:], b[:16], b[16:]], axis=1)


def alpha_kernel(arrived, inner, alpha, lower_inverse, out):
    total = jnp.sum(arrived[...], axis=0)
    mid_q, mid_r = total[:, :32], total[:, 32:64]
    gram, proj = total[:, 64:96], total[:, 96:]
    row = lax.broadcasted_iota(jnp.int32, (K, K), 0)
    column = lax.broadcasted_iota(jnp.int32, (K, K), 1)
    eye = (row == column).astype(jnp.float32)
    work = jnp.concatenate([gram, eye], axis=1)
    below = lax.broadcasted_iota(jnp.int32, (K, 1), 0)
    scale = jnp.zeros((K, 1), jnp.float32)
    for j in range(K):
        pivot = work[j : j + 1, j : j + 1]
        factor = jnp.where(below > j, work[:, j : j + 1] / pivot, 0.0)
        scale = jnp.where(below == j, lax.rsqrt(pivot), scale)
        work = work - factor * work[j : j + 1, :]
    inverse = work[:, K:] * scale
    mix = dot(inverse, dot(inverse, proj), ((0,), (0,)))
    alpha[...] = mix
    lower_inverse[...] = inverse
    coarse_mid = mid_r - dot(mid_q, mix)
    cross = inner[:, K:] - dot(inner[:, :K], mix) + dot(mid_q, coarse_mid, ((0,), (0,)))
    packed = packed4(coarse_mid, cross)
    for g in range(16):
        out[g] = packed


def sol_kernel(gathered, factor, out):
    cross = jnp.sum(gathered[...], axis=0)[:, 64:]
    mid = jnp.concatenate([gathered[g][:, h : h + K] for g in range(16) for h in (0, K)], axis=0)
    sol = dot(factor[...].reshape(512, 512), mid)
    for g in range(16):
        at = g * K
        out[g] = jnp.concatenate([sol[at : at + 16], sol[at + 16 : at + K], cross], axis=1)


def update_kernel(s, p, r, q, lined, alpha, new_s, new_r, local):
    mix = alpha[...]
    narrow(wide(s) + dot(mix, wide(p), ((0,), (0,))), new_s)
    narrow(wide(r) - dot(mix, q[...], ((0,), (0,))), new_r)
    local[...] = lined[pl.ds(K, K), :] - dot(mix, lined[pl.ds(0, K), :], ((0,), (0,)))


def direction_kernel(arrived, lower_inverse, local, basis, p, new_p, both):
    total = jnp.sum(arrived[...], axis=0)
    sol = jnp.concatenate([total[:, :32], total[:, 32:64]], axis=0)
    cross = jnp.concatenate([total[:, 64:96], total[:, 96:]], axis=0)
    inverse = lower_inverse[...]
    beta = -dot(inverse, dot(inverse, cross), ((0,), (0,)))
    mix = jnp.concatenate([sol, beta], axis=0)
    for f in range(F):
        columns = pl.ds(f * LANES, LANES)
        both[pl.ds(0, K), columns] = line(basis, f)
        both[pl.ds(K, K), columns] = line(p, f)
    narrow(local[...] + dot(mix, both[...], ((0,), (0,))), new_p)


def swapped(array, axes):
    return lax.all_to_all(array, axes, 0, 0, tiled=True)


def on_device(solution, residual, direction, mass, coarse_basis, line_inverse, coarse_factor):
    shape = direction.shape
    s, r, p, basis = (a.reshape(-1, LANES) for a in (solution, residual, direction, coarse_basis))
    inverse = line_inverse[0, 0]
    rows, length = p.shape
    flat = (K, F * LANES)

    slabs = call(slab_kernel, [(rows // 2, LANES)] * 4, name="halo_slabs")(p)
    low_x, high_x, low_y, high_y = slabs
    up_sub = [(i, i + 1) for i in range(63)]
    up_inner = [(i, i + 1) for i in range(3)]
    below_y = lax.ppermute(high_y, "x", up_inner)
    above_y = lax.ppermute(low_y, "x", [(b, a) for a, b in up_inner])
    below_x = lax.ppermute(high_x, SUB, up_sub)
    above_x = lax.ppermute(low_x, SUB, [(b, a) for a, b in up_sub])

    blocks = jnp.swapaxes(coarse_factor.reshape(32, 16, 512), 0, 1)
    factor = swapped(blocks, ROWS)
    (lined_r,) = call(lined_kernel, [(rows, LANES)], flops=50_000_000, name="lined_residual")(r, inverse)

    q, sums = call(
        image_kernel,
        [flat, (16, K, LANES)],
        [pltpu.VMEM((2 * K, F * LANES), jnp.float32)] * 2,
        name="image",
    )(p, r, basis, mass.reshape(16, LANES), below_x, above_x, below_y, above_y)
    gathered = swapped(sums, ROWS)
    lined, inner = call(
        image_lined_kernel,
        [(2 * K, F * LANES), (K, 2 * K)],
        [pltpu.VMEM((rows, LANES), jnp.float32)],
        flops=50_000_000,
        name="lined_image",
    )(q, lined_r, inverse)
    (parts,) = call(mid_kernel, [(16, K, LANES)], name="coarse_mid")(gathered, factor)
    arrived = swapped(parts, COLS)
    alpha, lower_inverse, spread = call(alpha_kernel, [(K, K), (K, K), (16, 16, LANES)], name="alpha")(arrived, inner)
    mids = swapped(spread, COLS)
    new_s, new_r, local = call(update_kernel, [(rows, LANES)] * 2 + [flat], flops=50_000_000, name="updates")(
        s, p, r, q, lined, alpha
    )
    (sols,) = call(sol_kernel, [(16, 16, LANES)], name="coarse_sol")(mids, factor)
    last = swapped(sols, ROWS)
    (new_p,) = call(
        direction_kernel, [(rows, LANES)], [pltpu.VMEM((2 * K, F * LANES), jnp.float32)], name="new_direction"
    )(last, lower_inverse, local, basis, p)
    return new_s.reshape(shape), new_r.reshape(shape), new_p.reshape(shape)


def solution(mesh):
    torus = Mesh(mesh.devices.reshape(8, 4, 2, 4), ("z", "y", "core", "x"))
    field = P(None, None, SUB, "x", None)
    return jax.shard_map(
        on_device,
        mesh=torus,
        in_specs=(field, field, field, P(SUB, "x", None), field, P(SUB, "x", None, None), P(SUB + ("x",), None)),
        out_specs=(field, field, field),
        check_vma=False,
    )
```

profile of v0, /device:TPU:1, one launch (start us, length us, event | category | flops | bytes accessed | tf_op | source)
XLA Modules:
  0.0 120.3 jit_solution(2805838397842374169)
XLA Ops:
  2.3 4.6 %collective-permute-start = (f32[768,128]{1,0:T(8,128)S(1)}, f32[768,128]{1,0:T(8,128)S(1)}, u32[]{:S(2)}, u32[]{:S(2)}) collective-permute-start(f32[768,128]{1,0:T(8,128)S(1)} %get-tuple-element.17), channel_id=1, source_target_pairs={{0,4},{4,8},{8,12},{12,16},{16,20},{20,24},{24,28},{28,32},{32,36}... | collective-permute-start | bytes 1179656 | tf_op jit(solution)/shard_map/ppermute | solution.py:217
  6.9 1.9 %collective-permute-start.1 = (f32[768,128]{1,0:T(8,128)S(1)}, f32[768,128]{1,0:T(8,128)S(1)}, u32[]{:S(2)}, u32[]{:S(2)}) collective-permute-start(f32[768,128]{1,0:T(8,128)S(1)} %get-tuple-element.18), channel_id=1, source_target_pairs={{4,0},{8,4},{12,8},{16,12},{20,16},{24,20},{28,24},{32,28},{36,32}... | collective-permute-start | bytes 1179656 | tf_op jit(solution)/shard_map/ppermute | solution.py:218
  8.8 3.1 %collective-permute-start.2 = (f32[768,128]{1,0:T(8,128)S(1)}, f32[768,128]{1,0:T(8,128)S(1)}, u32[]{:S(2)}, u32[]{:S(2)}) collective-permute-start(f32[768,128]{1,0:T(8,128)S(1)} %get-tuple-element.19), channel_id=1, source_target_pairs={{0,1},{1,2},{2,3},{4,5},{5,6},{6,7},{8,9},{9,10},{10,11},{12,13},{... | collective-permute-start | bytes 1179656 | tf_op jit(solution)/shard_map/ppermute | solution.py:215
  11.9 1.3 %collective-permute-start.3 = (f32[768,128]{1,0:T(8,128)S(1)}, f32[768,128]{1,0:T(8,128)S(1)}, u32[]{:S(2)}, u32[]{:S(2)}) collective-permute-start(f32[768,128]{1,0:T(8,128)S(1)} %get-tuple-element.20), channel_id=1, source_target_pairs={{1,0},{2,1},{3,2},{5,4},{6,5},{7,6},{9,8},{10,9},{11,10},{13,12},{... | collective-permute-start | bytes 1179656 | tf_op jit(solution)/shard_map/ppermute | solution.py:216
  13.2 3.0 %collective-permute-done.1.above_x = f32[768,128]{1,0:T(8,128)S(1)} collective-permute-done((f32[768,128]{1,0:T(8,128)S(1)}, f32[768,128]{1,0:T(8,128)S(1)}, u32[]{:S(2)}, u32[]{:S(2)}) %collective-permute-start.1) | collective-permute-done | bytes 393248 | tf_op jit(solution)/shard_map/ppermute | solution.py:218
  16.2 3.1 %collective-permute-done.2.below_y = f32[768,128]{1,0:T(8,128)S(1)} collective-permute-done((f32[768,128]{1,0:T(8,128)S(1)}, f32[768,128]{1,0:T(8,128)S(1)}, u32[]{:S(2)}, u32[]{:S(2)}) %collective-permute-start.2) | collective-permute-done | bytes 393248 | tf_op jit(solution)/shard_map/ppermute | solution.py:215
  19.3 4.1 %collective-permute-done.3.above_y = f32[768,128]{1,0:T(8,128)S(1)} collective-permute-done((f32[768,128]{1,0:T(8,128)S(1)}, f32[768,128]{1,0:T(8,128)S(1)}, u32[]{:S(2)}, u32[]{:S(2)}) %collective-permute-start.3) | collective-permute-done | bytes 393248 | tf_op jit(solution)/shard_map/ppermute | solution.py:216
  26.4 2.9 %image.1 = (f32[32,6144]{1,0:T(8,128)S(1)}, f32[16,32,128]{2,1,0:T(8,128)}) custom-call(f32[1536,128]{1,0:T(8,128)S(1)} %bitcast.17, f32[1536,128]{1,0:T(8,128)S(1)} %bitcast.20, f32[1536,128]{1,0:T(8,128)S(1)} %bitcast.23, f32[16,128]{1,0:T(8,128)S(1)} %bitcast.28, f32[768,128]{1,0:T(8,128)S(1)} %collective-permute-done.below_x, ...), custom_call_target="tpu_custom_call" | custom-call | flops 10000000 | bytes 4988928 | tf_op jit(solution)/shard_map/image/pallas_call | solution.py:45
  29.3 6.4 %all-to-all-start = ((f32[16,32,128]{2,1,0:T(8,128)}), f32[16,32,128]{2,1,0:T(8,128)S(1)}, u32[]{:S(2)}, u32[]{:S(2)}) async-start(f32[16,32,128]{2,1,0:T(8,128)} %get-tuple-element.23), calls=%async_computation | async-start | bytes 524288 | tf_op jit(solution)/shard_map/all_to_all | solution.py:201
  36.9 6.4 %all-to-all-done.gathered = f32[16,32,128]{2,1,0:T(8,128)S(1)} async-done(((f32[16,32,128]{2,1,0:T(8,128)}), f32[16,32,128]{2,1,0:T(8,128)S(1)}, u32[]{:S(2)}, u32[]{:S(2)}) %all-to-all-start) | async-done | bytes 262176 | tf_op jit(solution)/shard_map/all_to_all | solution.py:201
  43.3 17.5 %all_to_all.25.factor = f32[16,32,512]{2,1,0:T(8,128)S(1)} all-to-all(f32[16,32,512]{2,1,0:T(8,128)} %bitcast.29), channel_id=1, replica_groups=mesh['z'=8,'y'=4,'core'=2,'x'=4] {'y','x'}, dimensions={0} | all-to-all | bytes 2097152 | tf_op jit(solution)/shard_map/all_to_all | solution.py:201
  60.8 1.6 %coarse_mid.1 = f32[16,32,128]{2,1,0:T(8,128)} custom-call(f32[16,32,128]{2,1,0:T(8,128)S(1)} %all-to-all-done.gathered, f32[16,32,512]{2,1,0:T(8,128)S(1)} %all_to_all.25.factor), custom_call_target="tpu_custom_call" | custom-call | flops 10000000 | bytes 1572864 | tf_op jit(solution)/shard_map/coarse_mid/pallas_call | solution.py:45
  62.4 13.1 %all-to-all-start.2 = ((f32[16,32,128]{2,1,0:T(8,128)}), f32[16,32,128]{2,1,0:T(8,128)}, u32[]{:S(2)}, u32[]{:S(2)}) async-start(f32[16,32,128]{2,1,0:T(8,128)} %coarse_mid.1), calls=%async_computation.2 | async-start | bytes 524288 | tf_op jit(solution)/shard_map/all_to_all | solution.py:201
  76.3 3.2 %lined_image.1 = (f32[64,6144]{1,0:T(8,128)S(1)}, f32[32,64]{1,0:T(8,128)S(1)}) custom-call(f32[32,6144]{1,0:T(8,128)S(1)} %get-tuple-element.21.q, f32[1536,128]{1,0:T(8,128)S(1)} %lined_residual.1.lined_r, f32[128,128]{1,0:T(8,128)S(1)} %bitcast.27), custom_call_target="tpu_custom_call" | custom-call | flops 50000000 | bytes 3219456 | tf_op jit(solution)/shard_map/lined_image/pallas_call | solution.py:45
  79.6 1.2 copy-done.6
  80.7 6.6 %all-to-all-done.2.arrived = f32[16,32,128]{2,1,0:T(8,128)} async-done(((f32[16,32,128]{2,1,0:T(8,128)}), f32[16,32,128]{2,1,0:T(8,128)}, u32[]{:S(2)}, u32[]{:S(2)}) %all-to-all-start.2) | async-done | bytes 262176 | tf_op jit(solution)/shard_map/all_to_all | solution.py:201
  87.3 4.8 %alpha.1 = (f32[32,32]{1,0:T(8,128)S(1)}, f32[32,32]{1,0:T(8,128)S(1)}, f32[16,16,128]{2,1,0:T(8,128)S(1)}) custom-call(f32[16,32,128]{2,1,0:T(8,128)} %all-to-all-done.2.arrived, f32[32,64]{1,0:T(8,128)S(1)} %get-tuple-element.24.inner), custom_call_target="tpu_custom_call" | custom-call | flops 10000000 | bytes 409600 | tf_op jit(solution)/shard_map/alpha/pallas_call | solution.py:45
  92.1 11.9 %all_to_all.26.gathered = f32[16,16,128]{2,1,0:T(8,128)S(1)} all-to-all(f32[16,16,128]{2,1,0:T(8,128)S(1)} %get-tuple-element.28), channel_id=1, replica_groups=mesh['z'=8,'y'=4,'core'=2,'x'=4] {'z','core'}, dimensions={0} | all-to-all | bytes 262144 | tf_op jit(solution)/shard_map/all_to_all | solution.py:201
  104.0 1.8 %coarse_sol.1 = f32[16,16,128]{2,1,0:T(8,128)} custom-call(f32[16,16,128]{2,1,0:T(8,128)S(1)} %all_to_all.26.gathered, f32[16,32,512]{2,1,0:T(8,128)S(1)} %all_to_all.25.factor), custom_call_target="tpu_custom_call" | custom-call | flops 10000000 | bytes 1310720 | tf_op jit(solution)/shard_map/coarse_sol/pallas_call | solution.py:45
  105.8 3.7 %all-to-all-start.4 = ((f32[16,16,128]{2,1,0:T(8,128)}), f32[16,16,128]{2,1,0:T(8,128)S(1)}, u32[]{:S(2)}, u32[]{:S(2)}) async-start(f32[16,16,128]{2,1,0:T(8,128)} %coarse_sol.1), calls=%async_computation.4 | async-start | bytes 262144 | tf_op jit(solution)/shard_map/all_to_all | solution.py:201
  109.5 1.4 %copy-done.7 = f32[64,6144]{1,0:T(8,128)S(1)} copy-done((f32[64,6144]{1,0:T(8,128)S(1)}, f32[64,6144]{1,0:T(8,128)}, u32[]{:S(2)}) %copy-start.7) | copy-done | bytes 1572888
  112.0 2.6 %updates.1 = (f32[1536,128]{1,0:T(8,128)}, f32[1536,128]{1,0:T(8,128)}, f32[32,6144]{1,0:T(8,128)S(1)}) custom-call(f32[1536,128]{1,0:T(8,128)S(1)} %bitcast.25, f32[1536,128]{1,0:T(8,128)S(1)} %bitcast.18, f32[1536,128]{1,0:T(8,128)S(1)} %bitcast.22, f32[32,6144]{1,0:T(8,128)S(1)} %get-tuple-element.21.q, f32[64,6144]{1,0:T(8,128)S(1)} %copy-done.7, ...), custom_call_target="tpu_custom_call" | custom-call | flops 50000000 | bytes 7081984 | tf_op jit(solution)/shard_map/updates/pallas_call | solution.py:45
  115.5 1.2 all-to-all-done.4.arrived
  117.8 2.5 %new_direction.1 = f32[1536,128]{1,0:T(8,128)} custom-call(f32[16,16,128]{2,1,0:T(8,128)S(1)} %all-to-all-done.4.arrived, f32[32,32]{1,0:T(8,128)S(1)} %get-tuple-element.29.lower_inverse, f32[32,6144]{1,0:T(8,128)S(1)} %copy-done.10, f32[1536,128]{1,0:T(8,128)S(1)} %bitcast.24, f32[1536,128]{1,0:T(8,128)S(1)} %bitcast.19), custom_call_target="tpu_custom_call" | custom-call | flops 10000000 | bytes 3280896 | tf_op jit(solution)/shard_map/new_direction/pallas_call | solution.py:45
  (30 shorter events, 9.6 us)
Async XLA Ops:
  0.6 1.1 copy-start
  2.3 11.0 %collective-permute-start = (f32[768,128]{1,0:T(8,128)S(1)}, f32[768,128]{1,0:T(8,128)S(1)}, u32[]{:S(2)}, u32[]{:S(2)}) collective-permute-start(f32[768,128]{1,0:T(8,128)S(1)} %get-tuple-element.17), channel_id=1, source_target_pairs={{0,4},{4,8},{8,12},{12,16},{16,20},{20,24},{24,28},{28,32},{32,36}... | collective-permute-start | bytes 1179656 | tf_op jit(solution)/shard_map/ppermute | solution.py:217
  6.9 9.4 %collective-permute-start.1 = (f32[768,128]{1,0:T(8,128)S(1)}, f32[768,128]{1,0:T(8,128)S(1)}, u32[]{:S(2)}, u32[]{:S(2)}) collective-permute-start(f32[768,128]{1,0:T(8,128)S(1)} %get-tuple-element.18), channel_id=1, source_target_pairs={{4,0},{8,4},{12,8},{16,12},{20,16},{24,20},{28,24},{32,28},{36,32}... | collective-permute-start | bytes 1179656 | tf_op jit(solution)/shard_map/ppermute | solution.py:218
  8.8 10.5 %collective-permute-start.2 = (f32[768,128]{1,0:T(8,128)S(1)}, f32[768,128]{1,0:T(8,128)S(1)}, u32[]{:S(2)}, u32[]{:S(2)}) collective-permute-start(f32[768,128]{1,0:T(8,128)S(1)} %get-tuple-element.19), channel_id=1, source_target_pairs={{0,1},{1,2},{2,3},{4,5},{5,6},{6,7},{8,9},{9,10},{10,11},{12,13},{... | collective-permute-start | bytes 1179656 | tf_op jit(solution)/shard_map/ppermute | solution.py:215
  11.9 11.5 %collective-permute-start.3 = (f32[768,128]{1,0:T(8,128)S(1)}, f32[768,128]{1,0:T(8,128)S(1)}, u32[]{:S(2)}, u32[]{:S(2)}) collective-permute-start(f32[768,128]{1,0:T(8,128)S(1)} %get-tuple-element.20), channel_id=1, source_target_pairs={{1,0},{2,1},{3,2},{5,4},{6,5},{7,6},{9,8},{10,9},{11,10},{13,12},{... | collective-permute-start | bytes 1179656 | tf_op jit(solution)/shard_map/ppermute | solution.py:216
  23.4 1.1 copy-start.2
  24.6 1.1 copy-start.4
  25.7 0.7 copy-start.12
  26.4 9.3 %copy-start.13 = (f32[32,8192]{1,0:T(8,128)S(1)}, f32[32,8192]{1,0:T(8,128)}, u32[]{:S(2)}) copy-start(f32[32,8192]{1,0:T(8,128)} %param.13) | copy-start | bytes 3145732
  29.3 14.0 %all-to-all-start = ((f32[16,32,128]{2,1,0:T(8,128)}), f32[16,32,128]{2,1,0:T(8,128)S(1)}, u32[]{:S(2)}, u32[]{:S(2)}) async-start(f32[16,32,128]{2,1,0:T(8,128)} %get-tuple-element.23), calls=%async_computation | async-start | bytes 524288 | tf_op jit(solution)/shard_map/all_to_all | solution.py:201
  60.8 14.8 %copy-start.3 = (f32[32,3,4,4,128]{4,3,2,1,0:T(4,128)S(1)}, f32[32,3,4,4,128]{4,3,2,1,0:T(4,128)}, u32[]{:S(2)}) copy-start(f32[32,3,4,4,128]{4,3,2,1,0:T(4,128)} %param.8) | copy-start | bytes 2359300
  60.8 14.8 %copy-start.11 = (f32[1,1,128,128]{3,2,1,0:T(8,128)S(1)}, f32[1,1,128,128]{3,2,1,0:T(8,128)}, u32[]{:S(2)}) copy-start(f32[1,1,128,128]{3,2,1,0:T(8,128)} %param.12) | copy-start | bytes 196612
  62.4 24.9 %all-to-all-start.2 = ((f32[16,32,128]{2,1,0:T(8,128)}), f32[16,32,128]{2,1,0:T(8,128)}, u32[]{:S(2)}, u32[]{:S(2)}) async-start(f32[16,32,128]{2,1,0:T(8,128)} %coarse_mid.1), calls=%async_computation.2 | async-start | bytes 524288 | tf_op jit(solution)/shard_map/all_to_all | solution.py:201
  76.3 33.2 %copy-start.1 = (f32[32,3,4,4,128]{4,3,2,1,0:T(4,128)S(1)}, f32[32,3,4,4,128]{4,3,2,1,0:T(4,128)}, u32[]{:S(2)}) copy-start(f32[32,3,4,4,128]{4,3,2,1,0:T(4,128)} %param.9) | copy-start | bytes 2359300
  79.6 1.2 copy-start.6
  105.8 10.9 %all-to-all-start.4 = ((f32[16,16,128]{2,1,0:T(8,128)}), f32[16,16,128]{2,1,0:T(8,128)S(1)}, u32[]{:S(2)}, u32[]{:S(2)}) async-start(f32[16,16,128]{2,1,0:T(8,128)} %coarse_sol.1), calls=%async_computation.4 | async-start | bytes 262144 | tf_op jit(solution)/shard_map/all_to_all | solution.py:201
  109.5 1.4 %copy-start.7 = (f32[64,6144]{1,0:T(8,128)S(1)}, f32[64,6144]{1,0:T(8,128)}, u32[]{:S(2)}) copy-start(f32[64,6144]{1,0:T(8,128)} %copy-done.6) | copy-start | bytes 4718596
  110.9 1.1 copy-start.8
  112.0 4.7 %copy-start.5 = (f32[32,3,4,4,128]{4,3,2,1,0:T(4,128)S(1)}, f32[32,3,4,4,128]{4,3,2,1,0:T(4,128)}, u32[]{:S(2)}) copy-start(f32[32,3,4,4,128]{4,3,2,1,0:T(4,128)} %param.11) | copy-start | bytes 2359300
  114.6 0.9 copy-start.9
  116.7 1.1 copy-start.10
where the time goes:
time: 121 us; the launch traced here: 120 us
  starting transfers between devices  34.2 us (28%)
  blocking collectives  29.3 us (24%)
  waiting for transfers between devices  24.4 us (20%)
  Pallas kernels  20.6 us (17%)
  local copies, waits for them, and re-layouts  11 us (9%)
    all_to_all x2, blocking collectives, swapped(): return lax.all_to_all(array, axes, 0, 0, tiled=True)  29.3 us
    all_to_all x3, starting transfers between devices, swapped(): return lax.all_to_all(array, axes, 0, 0, tiled=True)  23.2 us
    pallas_call x9, Pallas kernels, run(): pl.pallas_call(kernel, out_shape=[jax.ShapeDtypeStruct(o, jnp.float32) fo...  20.6 us
    all_to_all x3, waiting for transfers between devices, swapped(): return lax.all_to_all(array, axes, 0, 0, tiled=True)  14.2 us
    unnamed x28, local copies, waits for them, and re-layouts  9.85 us
    ppermute x1, starting transfers between devices, on_device(): below_x = lax.ppermute(high_x, SUB, up_sub)  4.59 us
    ppermute x1, waiting for transfers between devices, on_device(): above_y = lax.ppermute(low_y, 'x', [(b, a) for a, b in up_inner])  4.12 us
    ppermute x1, starting transfers between devices, on_device(): below_y = lax.ppermute(high_y, 'x', up_inner)  3.14 us
  transfers between devices with their start and end apart: 7, of which 6 were waited for; matrix products, arithmetic and copies ran while one was open for 1% of the time, Pallas kernels for 5%

commit v1 on v0

v1 whole, which is shorter than its diff:
```python
import jax
import jax.numpy as jnp
from jax import lax
from jax.experimental import pallas as pl
from jax.experimental.pallas import tpu as pltpu
from jax.sharding import Mesh
from jax.sharding import PartitionSpec as P

SUB = ("z", "y", "core")
ROWS = ("y", "x")
COLS = ("z", "core")
exact = lax.Precision.HIGHEST

K = 32
F = 48
LANES = 128


def dot(a, b, dims=((1,), (0,))):
    return lax.dot_general(a, b, (dims, ((), ())), precision=exact, preferred_element_type=jnp.float32)


def line(ref, f):
    return ref[pl.ds(f, K, stride=F), :]


def place(c, x, y):
    return (c * 4 + x) * 4 + y


def wide(ref):
    return jnp.concatenate([line(ref, f) for f in range(F)], axis=1)


def narrow(value, ref):
    for f in range(F):
        ref[pl.ds(f, K, stride=F), :] = value[:, f * LANES : (f + 1) * LANES]


def call(kernel, outs, fetched, stored, scratch=(), flops=10_000_000, unread=0, name=None, held=0):
    def run(*args):
        n, m = len(args), len(outs)
        whole = n - unread - fetched
        vmem, hbm = pl.BlockSpec(memory_space=pltpu.VMEM), pl.BlockSpec(memory_space=pltpu.HBM)

        def body(*refs):
            given, made, own = refs[:n], refs[n : n + m], refs[n + m :]
            buffers, semaphores = own[: fetched + stored], own[fetched + stored : 2 * (fetched + stored)]
            rest = own[2 * (fetched + stored) :]
            fetches = [
                pltpu.make_async_copy(*three) for three in zip(given[:fetched], buffers[:fetched], semaphores[:fetched])
            ]
            stores = [
                pltpu.make_async_copy(*three) for three in zip(buffers[fetched:], made[:stored], semaphores[fetched:])
            ]
            for fetch in fetches:
                fetch.start()
            kernel(
                lambda i: fetches[i].wait(),
                lambda i: stores[i].start(),
                *buffers[:fetched],
                *given[fetched : fetched + whole],
                *buffers[fetched:],
                *made[stored:],
                *rest,
            )
            for store in stores:
                store.wait()

        sizes = [a.size for a in args[: fetched + whole]]
        for o in outs:
            sizes.append(1)
            for length in o:
                sizes[-1] *= length
        return pl.pallas_call(
            body,
            out_shape=[pltpu.HBM(o, jnp.float32) for o in outs[:stored]]
            + [jax.ShapeDtypeStruct(o, jnp.float32) for o in outs[stored:]],
            in_specs=[hbm] * fetched + [vmem] * whole + [hbm] * unread,
            out_specs=[hbm] * stored + [vmem] * (m - stored),
            scratch_shapes=[pltpu.VMEM(a.shape, jnp.float32) for a in args[:fetched]]
            + [pltpu.VMEM(o, jnp.float32) for o in outs[:stored]]
            + [pltpu.SemaphoreType.DMA] * (fetched + stored)
            + [pltpu.VMEM(shape, jnp.float32) for shape in scratch],
            compiler_params=pltpu.CompilerParams(vmem_limit_bytes=24 * 1024 * 1024),
            cost_estimate=pl.CostEstimate(flops=flops, bytes_accessed=4 * sum(sizes), transcendentals=0),
            name=name,
            )(
            *(pltpu.with_memory_space_constraint(a, pltpu.HBM) for a in args[:fetched]),
            *(pltpu.with_memory_space_constraint(a, pltpu.VMEM) for a in args[fetched : fetched + held]),
            *args[fetched + held :],
        )

    return run


def slab_kernel(wait, put, p, low_x, high_x, low_y, high_y):
    wait(0)
    at = 0
    for c in range(3):
        for x in range(2):
            for y in range(4):
                low_x[pl.ds(at * K, K), :] = line(p, place(c, x, y))
                high_x[pl.ds(at * K, K), :] = line(p, place(c, x + 2, y))
                at += 1
    put(0)
    put(1)
    at = 0
    for c in range(3):
        for x in range(4):
            for y in range(2):
                low_y[pl.ds(at * K, K), :] = line(p, place(c, x, y))
                high_y[pl.ds(at * K, K), :] = line(p, place(c, x, y + 2))
                at += 1
    put(2)
    put(3)


def residual_sums_kernel(wait, put, p, basis, r, sums, left):
    wait(0)
    wait(1)
    for f in range(F):
        columns = pl.ds(f * LANES, LANES)
        left[pl.ds(0, K), columns] = line(p, f)
        left[pl.ds(K, K), columns] = line(basis, f)
    wait(2)
    sums[...] = dot(left[...], wide(r), ((1,), (1,)))


def image_kernel(wait, put, p, basis, mass, below_x, above_x, below_y, above_y, sums_r, q, sums, left):
    lane = lax.broadcasted_iota(jnp.int32, (K, LANES), 1)

    def at(c, x, y):
        if x < 0:
            return below_x[pl.ds(((c * 2 + x + 2) * 4 + y) * K, K), :]
        if x > 3:
            return above_x[pl.ds(((c * 2 + x - 4) * 4 + y) * K, K), :]
        if y < 0:
            return below_y[pl.ds(((c * 4 + x) * 2 + y + 2) * K, K), :]
        if y > 3:
            return above_y[pl.ds(((c * 4 + x) * 2 + y - 4) * K, K), :]
        return left[pl.ds(0, K), pl.ds(place(c, x, y) * LANES, LANES)]

    wait(0)
    for f in range(F):
        left[pl.ds(0, K), pl.ds(f * LANES, LANES)] = line(p, f)
    wait(2)
    for c in range(3):
        for x in range(4):
            for y in range(4):
                f = place(c, x, y)
                center = at(c, x, y)
                near = at(c, x - 1, y) + at(c, x + 1, y) + at(c, x, y - 1) + at(c, x, y + 1)
                far = at(c, x - 2, y) + at(c, x + 2, y) + at(c, x, y - 2) + at(c, x, y + 2)
                near = near + jnp.where(lane >= 1, pltpu.roll(center, 1, 1), 0.0)
                near = near + jnp.where(lane < LANES - 1, pltpu.roll(center, LANES - 1, 1), 0.0)
                far = far + jnp.where(lane >= 2, pltpu.roll(center, 2, 1), 0.0)
                far = far + jnp.where(lane < LANES - 2, pltpu.roll(center, LANES - 2, 1), 0.0)
                weight = mass[pl.ds(x * 4 + y, 1), :] + 7.5
                q[:, pl.ds(f * LANES, LANES)] = weight * center - (4.0 / 3.0) * near + (1.0 / 12.0) * far
    put(0)
    wait(1)
    for f in range(F):
        left[pl.ds(K, K), pl.ds(f * LANES, LANES)] = line(basis, f)
    sums_q = dot(left[...], q[...], ((1,), (1,)))
    packed = jnp.concatenate([sums_q[:K], sums_r[:K], sums_q[K:], sums_r[K:]], axis=1)
    for g in range(16):
        sums[g] = packed


def image_lined_kernel(wait, put, q, inverse, r, inner, lines, right):
    wait(0)
    for f in range(F):
        lines[pl.ds(f * K, K), :] = q[:, pl.ds(f * LANES, LANES)]
    wait(2)
    for f in range(F):
        lines[pl.ds((F + f) * K, K), :] = line(r, f)
    wait(1)
    lines[...] = dot(lines[...], inverse[...], ((1,), (1,)))
    for f in range(F):
        columns = pl.ds(f * LANES, LANES)
        right[pl.ds(0, K), columns] = lines[pl.ds(f * K, K), :]
        right[pl.ds(K, K), columns] = lines[pl.ds((F + f) * K, K), :]
    inner[...] = dot(q[...], right[...], ((1,), (1,)))


def mid_kernel(wait, put, factor, gathered, out):
    total = jnp.sum(gathered[...], axis=0)
    rhs = jnp.concatenate([gathered[g][:, 64:] for g in range(16)], axis=0)
    mid = dot(rhs.T, factor[...].reshape(512, 512)).T
    for g in range(16):
        out[g] = jnp.concatenate([mid[g * K : (g + 1) * K], total[:, :64]], axis=1)


def packed4(a, b):
    return jnp.concatenate([a[:16], a[16:], b[:16], b[16:]], axis=1)


def alpha_kernel(wait, put, arrived, inner, alpha, lower_inverse, out):
    total = jnp.sum(arrived[...], axis=0)
    mid_q, mid_r = total[:, :32], total[:, 32:64]
    gram, proj = total[:, 64:96], total[:, 96:]
    row = lax.broadcasted_iota(jnp.int32, (K, K), 0)
    column = lax.broadcasted_iota(jnp.int32, (K, K), 1)
    eye = (row == column).astype(jnp.float32)
    work = jnp.concatenate([gram, eye], axis=1)
    below = lax.broadcasted_iota(jnp.int32, (K, 1), 0)
    scale = jnp.zeros((K, 1), jnp.float32)
    for j in range(K):
        pivot = work[j : j + 1, j : j + 1]
        factor = jnp.where(below > j, work[:, j : j + 1] / pivot, 0.0)
        scale = jnp.where(below == j, lax.rsqrt(pivot), scale)
        work = work - factor * work[j : j + 1, :]
    inverse = work[:, K:] * scale
    mix = dot(inverse, dot(inverse, proj), ((0,), (0,)))
    alpha[...] = mix
    lower_inverse[...] = inverse
    coarse_mid = mid_r - dot(mid_q, mix)
    cross = inner[:, K:] - dot(inner[:, :K], mix) + dot(mid_q, coarse_mid, ((0,), (0,)))
    packed = packed4(coarse_mid, cross)
    for g in range(16):
        out[g] = packed


def sol_kernel(wait, put, factor, gathered, out):
    cross = jnp.sum(gathered[...], axis=0)[:, 64:]
    mid = jnp.concatenate([gathered[g][:, h : h + K] for g in range(16) for h in (0, K)], axis=0)
    sol = dot(factor[...].reshape(512, 512), mid)
    for g in range(16):
        at = g * K
        out[g] = jnp.concatenate([sol[at : at + 16], sol[at + 16 : at + K], cross], axis=1)


def update_kernel(wait, put, q, r, inverse, s, p, alpha, new_s, new_r, local):
    mix = alpha[...]
    wait(0)
    wait(1)
    narrow(wide(r) - dot(mix, q[...], ((0,), (0,))), new_r)
    put(1)
    wait(2)
    local[...] = dot(new_r[...], inverse[...], ((1,), (1,)))
    put(2)
    wait(3)
    wait(4)
    narrow(wide(s) + dot(mix, wide(p), ((0,), (0,))), new_s)
    put(0)


def direction_kernel(wait, put, p, basis, local, arrived, lower_inverse, new_p, left):
    total = jnp.sum(arrived[...], axis=0)
    sol = jnp.concatenate([total[:, :32], total[:, 32:64]], axis=0)
    cross = jnp.concatenate([total[:, 64:96], total[:, 96:]], axis=0)
    inverse = lower_inverse[...]
    beta = -dot(inverse, dot(inverse, cross), ((0,), (0,)))
    mix = jnp.concatenate([beta, sol], axis=0)
    wait(0)
    wait(1)
    for f in range(F):
        columns = pl.ds(f * LANES, LANES)
        left[pl.ds(0, K), columns] = line(p, f)
        left[pl.ds(K, K), columns] = line(basis, f)
    change = dot(mix, left[...], ((0,), (0,)))
    wait(2)
    narrow(wide(local) + change, new_p)
    put(0)


def swapped(array, axes):
    return lax.all_to_all(array, axes, 0, 0, tiled=True)


def on_device(solution, residual, direction, mass, coarse_basis, line_inverse, coarse_factor):
    shape = direction.shape
    s, r, p, basis = (a.reshape(-1, LANES) for a in (solution, residual, direction, coarse_basis))
    inverse = line_inverse[0, 0]
    rows, length = p.shape
    flat = (K, F * LANES)

    slabs = call(slab_kernel, [(rows // 2, LANES)] * 4, 1, 4, name="halo_slabs")(p)
    low_x, high_x, low_y, high_y = slabs
    up_sub = [(i, i + 1) for i in range(63)]
    up_inner = [(i, i + 1) for i in range(3)]
    below_y = lax.ppermute(high_y, "x", up_inner)
    above_y = lax.ppermute(low_y, "x", [(b, a) for a, b in up_inner])
    below_x = lax.ppermute(high_x, SUB, up_sub)
    above_x = lax.ppermute(low_x, SUB, [(b, a) for a, b in up_sub])

    blocks = jnp.swapaxes(coarse_factor.reshape(32, 16, 512), 0, 1)
    factor = swapped(blocks, ROWS)
    double = (2 * K, F * LANES)
    (sums_r,) = call(residual_sums_kernel, [(2 * K, K)], 3, 0, [double], 25_000_000, name="residual_sums")(p, basis, r)
    q, sums = call(image_kernel, [flat, (16, K, LANES)], 3, 1, [double], 25_000_000, unread=1, held=4, name="image")(
        p, basis, mass.reshape(16, LANES), below_x, above_x, below_y, above_y, sums_r, factor
    )
    gathered = swapped(sums, ROWS)
    (inner,) = call(image_lined_kernel, [(K, 2 * K)], 3, 0, [(2 * rows, LANES), double], 125_000_000, name="lined_image")(
        q, inverse, r
    )
    (parts,) = call(mid_kernel, [(16, K, LANES)], 0, 0, held=1, name="coarse_mid")(factor, gathered)
    arrived = swapped(parts, COLS)
    alpha, lower_inverse, spread = call(alpha_kernel, [(K, K), (K, K), (16, 16, LANES)], 0, 0, name="alpha")(
        arrived, inner
    )
    mids = swapped(spread, COLS)
    new_s, new_r, local = call(update_kernel, [(rows, LANES)] * 3, 5, 3, flops=75_000_000, name="updates")(
        q, r, inverse, s, p, alpha
    )
    (sols,) = call(sol_kernel, [(16, 16, LANES)], 0, 0, held=1, name="coarse_sol")(factor, mids)
    last = swapped(sols, ROWS)
    (new_p,) = call(direction_kernel, [(rows, LANES)], 3, 1, [double], 25_000_000, name="new_direction")(
        p, basis, local, last, lower_inverse
    )
    return new_s.reshape(shape), new_r.reshape(shape), new_p.reshape(shape)


def solution(mesh):
    torus = Mesh(mesh.devices.reshape(8, 4, 2, 4), ("z", "y", "core", "x"))
    field = P(None, None, SUB, "x", None)
    return jax.shard_map(
        on_device,
        mesh=torus,
        in_specs=(field, field, field, P(SUB, "x", None), field, P(SUB, "x", None, None), P(SUB + ("x",), None)),
        out_specs=(field, field, field),
        check_vma=False,
    )
```

time: 121 us -> 110 us (0.909)
  Pallas kernels: 20.6 us -> 33.5 us
  waiting for transfers between devices: 24.4 us -> 13.3 us
  local copies, waits for them, and re-layouts: 11 us -> 2.29 us
  blocking collectives: 29.3 us -> 26.5 us
  starting transfers between devices: 34.2 us -> 32.6 us
    pallas_call x9, Pallas kernels: 20.6 us -> 33.5 us  [run(): pl.pallas_call(body, out_shape=[pltpu.HBM(o, jnp.float32) for o in outs[:...]
    unnamed x28 -> x0, local copies, waits for them, and re-layouts: 9.85 us -> none
    all_to_all x3, waiting for transfers between devices: 14.2 us -> 6.56 us  [swapped(): return lax.all_to_all(array, axes, 0, 0, tiled=True)]
    all_to_all x2, blocking collectives: 29.3 us -> 26.5 us  [swapped(): return lax.all_to_all(array, axes, 0, 0, tiled=True)]
    ppermute x1, waiting for transfers between devices: 3.08 us -> 1.55 us  [on_device(): below_y = lax.ppermute(high_y, 'x', up_inner)]
    all_to_all x3, starting transfers between devices: 23.2 us -> 21.8 us  [swapped(): return lax.all_to_all(array, axes, 0, 0, tiled=True)]
  transfers between devices with their start and end apart: 7 -> 7, of which waited for: 6 -> 5; matrix products, arithmetic and copies ran while one was open for 1% -> 0% of each run, Pallas kernels for 5% -> 17%
where the time goes in v1:
time: 110 us; the launch traced here: 109 us
  Pallas kernels  33.5 us (30%)
  starting transfers between devices  32.6 us (30%)
  blocking collectives  26.5 us (24%)
  waiting for transfers between devices  13.3 us (12%)
  local copies, waits for them, and re-layouts  2.29 us (2%)
    pallas_call x9, Pallas kernels, run(): pl.pallas_call(body, out_shape=[pltpu.HBM(o, jnp.float32) for o in outs[:...  33.5 us
    all_to_all x2, blocking collectives, swapped(): return lax.all_to_all(array, axes, 0, 0, tiled=True)  26.5 us
    all_to_all x3, starting transfers between devices, swapped(): return lax.all_to_all(array, axes, 0, 0, tiled=True)  21.8 us
    all_to_all x3, waiting for transfers between devices, swapped(): return lax.all_to_all(array, axes, 0, 0, tiled=True)  6.56 us
    ppermute x1, starting transfers between devices, on_device(): below_x = lax.ppermute(high_x, SUB, up_sub)  4.39 us
    ppermute x1, starting transfers between devices, on_device(): below_y = lax.ppermute(high_y, 'x', up_inner)  3.11 us
    ppermute x1, waiting for transfers between devices, on_device(): above_y = lax.ppermute(low_y, 'x', [(b, a) for a, b in up_inner])  2.98 us
    reshape x1, local copies, waits for them, and re-layouts, on_device(): blocks = jnp.swapaxes(coarse_factor.reshape(32, 16, 512), 0, 1)  2.29 us
  transfers between devices with their start and end apart: 7, of which 5 were waited for; matrix products, arithmetic and copies ran while one was open for 0% of the time, Pallas kernels for 17%

profile of v1, /device:TPU:1, one launch (start us, length us, event | category | flops | bytes accessed | tf_op | source)
XLA Modules:
  0.0 109.0 jit_solution(257294940033651126)
XLA Ops:
  0.6 2.3 %copy.13 = f32[4,16,8,512]{3,2,0,1:T(8,128)} copy(f32[4,16,8,512]{3,2,1,0:T(8,128)} %bitcast.27) | data formatting | bytes 2097152 | tf_op jit(solution)/shard_map/reshape | solution.py:288
  2.9 7.6 %all-to-all-start = ((f32[16,32,512]{2,1,0:T(8,128)}), f32[16,32,512]{2,1,0:T(8,128)S(1)}, u32[]{:S(2)}, u32[]{:S(2)}) async-start(f32[16,32,512]{2,1,0:T(8,128)} %bitcast.15), calls=%async_computation | async-start | bytes 2097152 | tf_op jit(solution)/shard_map/all_to_all | solution.py:269
  10.5 2.6 %halo_slabs.1 = (f32[768,128]{1,0:T(8,128)}, f32[768,128]{1,0:T(8,128)}, f32[768,128]{1,0:T(8,128)}, f32[768,128]{1,0:T(8,128)}) custom-call(f32[1536,128]{1,0:T(8,128)} %bitcast.16), custom_call_target="tpu_custom_call" | custom-call | flops 10000000 | bytes 2359296 | tf_op jit(solution)/shard_map/halo_slabs/pallas_call | solution.py:75
  13.1 4.4 %collective-permute-start = (f32[768,128]{1,0:T(8,128)}, f32[768,128]{1,0:T(8,128)S(1)}, u32[]{:S(2)}, u32[]{:S(2)}) collective-permute-start(f32[768,128]{1,0:T(8,128)} %get-tuple-element.15), channel_id=1, source_target_pairs={{0,4},{4,8},{8,12},{12,16},{16,20},{20,24},{24,28},{28,32},{32,36}... | collective-permute-start | bytes 1179656 | tf_op jit(solution)/shard_map/ppermute | solution.py:285
  17.5 1.9 %collective-permute-start.1 = (f32[768,128]{1,0:T(8,128)}, f32[768,128]{1,0:T(8,128)S(1)}, u32[]{:S(2)}, u32[]{:S(2)}) collective-permute-start(f32[768,128]{1,0:T(8,128)} %get-tuple-element.16), channel_id=1, source_target_pairs={{4,0},{8,4},{12,8},{16,12},{20,16},{24,20},{28,24},{32,28},{36,32}... | collective-permute-start | bytes 1179656 | tf_op jit(solution)/shard_map/ppermute | solution.py:286
  19.4 3.1 %collective-permute-start.2 = (f32[768,128]{1,0:T(8,128)}, f32[768,128]{1,0:T(8,128)S(1)}, u32[]{:S(2)}, u32[]{:S(2)}) collective-permute-start(f32[768,128]{1,0:T(8,128)} %get-tuple-element.17), channel_id=1, source_target_pairs={{0,1},{1,2},{2,3},{4,5},{5,6},{6,7},{8,9},{9,10},{10,11},{12,13},{... | collective-permute-start | bytes 1179656 | tf_op jit(solution)/shard_map/ppermute | solution.py:283
  22.5 1.3 %collective-permute-start.3 = (f32[768,128]{1,0:T(8,128)}, f32[768,128]{1,0:T(8,128)S(1)}, u32[]{:S(2)}, u32[]{:S(2)}) collective-permute-start(f32[768,128]{1,0:T(8,128)} %get-tuple-element.18), channel_id=1, source_target_pairs={{1,0},{2,1},{3,2},{5,4},{6,5},{7,6},{9,8},{10,9},{11,10},{13,12},{... | collective-permute-start | bytes 1179656 | tf_op jit(solution)/shard_map/ppermute | solution.py:284
  23.8 3.4 %residual_sums.1.refs_7_ = f32[64,32]{1,0:T(8,128)S(1)} custom-call(f32[1536,128]{1,0:T(8,128)} %bitcast.17, f32[1536,128]{1,0:T(8,128)} %bitcast.21, f32[1536,128]{1,0:T(8,128)} %bitcast.24), custom_call_target="tpu_custom_call" | custom-call | flops 25000000 | bytes 2367488 | tf_op jit(solution)/shard_map/residual_sums/pallas_call | solution.py:75
  27.2 2.2 %collective-permute-done.1.refs_4_ = f32[768,128]{1,0:T(8,128)S(1)} collective-permute-done((f32[768,128]{1,0:T(8,128)}, f32[768,128]{1,0:T(8,128)S(1)}, u32[]{:S(2)}, u32[]{:S(2)}) %collective-permute-start.1) | collective-permute-done | bytes 393248 | tf_op jit(solution)/shard_map/ppermute | solution.py:286
  29.4 1.6 %collective-permute-done.2.refs_5_ = f32[768,128]{1,0:T(8,128)S(1)} collective-permute-done((f32[768,128]{1,0:T(8,128)}, f32[768,128]{1,0:T(8,128)S(1)}, u32[]{:S(2)}, u32[]{:S(2)}) %collective-permute-start.2) | collective-permute-done | bytes 393248 | tf_op jit(solution)/shard_map/ppermute | solution.py:283
  30.9 3.0 %collective-permute-done.3.refs_6_ = f32[768,128]{1,0:T(8,128)S(1)} collective-permute-done((f32[768,128]{1,0:T(8,128)}, f32[768,128]{1,0:T(8,128)S(1)}, u32[]{:S(2)}, u32[]{:S(2)}) %collective-permute-start.3) | collective-permute-done | bytes 393248 | tf_op jit(solution)/shard_map/ppermute | solution.py:284
  33.9 3.8 %image.1 = (f32[32,6144]{1,0:T(8,128)}, f32[16,32,128]{2,1,0:T(8,128)S(1)}) custom-call(f32[1536,128]{1,0:T(8,128)} %bitcast.18, f32[1536,128]{1,0:T(8,128)} %bitcast.22, f32[16,128]{1,0:T(8,128)} %bitcast.32, f32[768,128]{1,0:T(8,128)S(1)} %collective-permute-done.refs_3_, f32[768,128]{1,0:T(8,128)S(1)} %collective-permute-done.1.refs_4_, ...), custom_call_target="tpu_custom_call" | custom-call | flops 25000000 | bytes 4210688 | tf_op jit(solution)/shard_map/image/pallas_call | solution.py:75
  37.8 14.6 %all_to_all.25.refs_1_ = f32[16,32,128]{2,1,0:T(8,128)S(1)} all-to-all(f32[16,32,128]{2,1,0:T(8,128)S(1)} %get-tuple-element.20), channel_id=1, replica_groups=mesh['z'=8,'y'=4,'core'=2,'x'=4] {'y','x'}, dimensions={0} | all-to-all | bytes 524288 | tf_op jit(solution)/shard_map/all_to_all | solution.py:269
  52.4 1.6 %coarse_mid.1 = f32[16,32,128]{2,1,0:T(8,128)} custom-call(f32[16,32,512]{2,1,0:T(8,128)S(1)} %all-to-all-done.refs_8_.refs_0_, f32[16,32,128]{2,1,0:T(8,128)S(1)} %all_to_all.25.refs_1_), custom_call_target="tpu_custom_call" | custom-call | flops 10000000 | bytes 1572864 | tf_op jit(solution)/shard_map/coarse_mid/pallas_call | solution.py:75
  54.0 10.7 %all-to-all-start.2 = ((f32[16,32,128]{2,1,0:T(8,128)}), f32[16,32,128]{2,1,0:T(8,128)S(1)}, u32[]{:S(2)}, u32[]{:S(2)}) async-start(f32[16,32,128]{2,1,0:T(8,128)} %coarse_mid.1), calls=%async_computation.2 | async-start | bytes 524288 | tf_op jit(solution)/shard_map/all_to_all | solution.py:269
  64.8 6.6 %lined_image.1.refs_1_ = f32[32,64]{1,0:T(8,128)S(1)} custom-call(f32[32,6144]{1,0:T(8,128)} %get-tuple-element.19.refs_0_, f32[128,128]{1,0:T(8,128)} %bitcast.30, f32[1536,128]{1,0:T(8,128)} %bitcast.25), custom_call_target="tpu_custom_call" | custom-call | flops 125000000 | bytes 1646592 | tf_op jit(solution)/shard_map/lined_image/pallas_call | solution.py:75
  71.4 5.1 %all-to-all-done.2.refs_0_ = f32[16,32,128]{2,1,0:T(8,128)S(1)} async-done(((f32[16,32,128]{2,1,0:T(8,128)}), f32[16,32,128]{2,1,0:T(8,128)S(1)}, u32[]{:S(2)}, u32[]{:S(2)}) %all-to-all-start.2) | async-done | bytes 262176 | tf_op jit(solution)/shard_map/all_to_all | solution.py:269
  76.5 3.8 %alpha.1 = (f32[32,32]{1,0:T(8,128)S(1)}, f32[32,32]{1,0:T(8,128)S(1)}, f32[16,16,128]{2,1,0:T(8,128)S(1)}) custom-call(f32[16,32,128]{2,1,0:T(8,128)S(1)} %all-to-all-done.2.refs_0_, f32[32,64]{1,0:T(8,128)S(1)} %lined_image.1.refs_1_), custom_call_target="tpu_custom_call" | custom-call | flops 10000000 | bytes 409600 | tf_op jit(solution)/shard_map/alpha/pallas_call | solution.py:75
  80.3 11.9 %all_to_all.26.refs_1_ = f32[16,16,128]{2,1,0:T(8,128)S(1)} all-to-all(f32[16,16,128]{2,1,0:T(8,128)S(1)} %get-tuple-element.25), channel_id=1, replica_groups=mesh['z'=8,'y'=4,'core'=2,'x'=4] {'z','core'}, dimensions={0} | all-to-all | bytes 262144 | tf_op jit(solution)/shard_map/all_to_all | solution.py:269
  92.2 1.8 %coarse_sol.1 = f32[16,16,128]{2,1,0:T(8,128)} custom-call(f32[16,32,512]{2,1,0:T(8,128)S(1)} %all-to-all-done.refs_8_.refs_0_, f32[16,16,128]{2,1,0:T(8,128)S(1)} %all_to_all.26.refs_1_), custom_call_target="tpu_custom_call" | custom-call | flops 10000000 | bytes 1310720 | tf_op jit(solution)/shard_map/coarse_sol/pallas_call | solution.py:75
  94.0 3.5 %all-to-all-start.4 = ((f32[16,16,128]{2,1,0:T(8,128)}), f32[16,16,128]{2,1,0:T(8,128)S(1)}, u32[]{:S(2)}, u32[]{:S(2)}) async-start(f32[16,16,128]{2,1,0:T(8,128)} %coarse_sol.1), calls=%async_computation.4 | async-start | bytes 262144 | tf_op jit(solution)/shard_map/all_to_all | solution.py:269
  97.5 5.9 %updates.1 = (f32[1536,128]{1,0:T(8,128)}, f32[1536,128]{1,0:T(8,128)}, f32[1536,128]{1,0:T(8,128)}) custom-call(f32[32,6144]{1,0:T(8,128)} %get-tuple-element.19.refs_0_, f32[1536,128]{1,0:T(8,128)} %bitcast.26, f32[128,128]{1,0:T(8,128)} %bitcast.31, f32[1536,128]{1,0:T(8,128)} %bitcast.28, f32[1536,128]{1,0:T(8,128)} %bitcast.19, ...), custom_call_target="tpu_custom_call" | custom-call | flops 75000000 | bytes 5574656 | tf_op jit(solution)/shard_map/updates/pallas_call | solution.py:75
  103.4 1.5 %all-to-all-done.4.refs_3_ = f32[16,16,128]{2,1,0:T(8,128)S(1)} async-done(((f32[16,16,128]{2,1,0:T(8,128)}), f32[16,16,128]{2,1,0:T(8,128)S(1)}, u32[]{:S(2)}, u32[]{:S(2)}) %all-to-all-start.4) | async-done | bytes 131104 | tf_op jit(solution)/shard_map/all_to_all | solution.py:269
  104.9 3.9 %new_direction.1 = f32[1536,128]{1,0:T(8,128)} custom-call(f32[1536,128]{1,0:T(8,128)} %bitcast.20, f32[1536,128]{1,0:T(8,128)} %bitcast.23, f32[1536,128]{1,0:T(8,128)} %get-tuple-element.24.refs_2_, f32[16,16,128]{2,1,0:T(8,128)S(1)} %all-to-all-done.4.refs_3_, f32[32,32]{1,0:T(8,128)S(1)} %get-tuple-element.26.refs_4_), custom_call_target="tpu_custom_call" | custom-call | flops 25000000 | bytes 3280896 | tf_op jit(solution)/shard_map/new_direction/pallas_call | solution.py:75
  (2 shorter events, 0.0 us)
Async XLA Ops:
  2.9 31.0 %all-to-all-start = ((f32[16,32,512]{2,1,0:T(8,128)}), f32[16,32,512]{2,1,0:T(8,128)S(1)}, u32[]{:S(2)}, u32[]{:S(2)}) async-start(f32[16,32,512]{2,1,0:T(8,128)} %bitcast.15), calls=%async_computation | async-start | bytes 2097152 | tf_op jit(solution)/shard_map/all_to_all | solution.py:269
  13.1 14.1 %collective-permute-start = (f32[768,128]{1,0:T(8,128)}, f32[768,128]{1,0:T(8,128)S(1)}, u32[]{:S(2)}, u32[]{:S(2)}) collective-permute-start(f32[768,128]{1,0:T(8,128)} %get-tuple-element.15), channel_id=1, source_target_pairs={{0,4},{4,8},{8,12},{12,16},{16,20},{20,24},{24,28},{28,32},{32,36}... | collective-permute-start | bytes 1179656 | tf_op jit(solution)/shard_map/ppermute | solution.py:285
  17.5 11.9 %collective-permute-start.1 = (f32[768,128]{1,0:T(8,128)}, f32[768,128]{1,0:T(8,128)S(1)}, u32[]{:S(2)}, u32[]{:S(2)}) collective-permute-start(f32[768,128]{1,0:T(8,128)} %get-tuple-element.16), channel_id=1, source_target_pairs={{4,0},{8,4},{12,8},{16,12},{20,16},{24,20},{28,24},{32,28},{36,32}... | collective-permute-start | bytes 1179656 | tf_op jit(solution)/shard_map/ppermute | solution.py:286
  19.4 11.5 %collective-permute-start.2 = (f32[768,128]{1,0:T(8,128)}, f32[768,128]{1,0:T(8,128)S(1)}, u32[]{:S(2)}, u32[]{:S(2)}) collective-permute-start(f32[768,128]{1,0:T(8,128)} %get-tuple-element.17), channel_id=1, source_target_pairs={{0,1},{1,2},{2,3},{4,5},{5,6},{6,7},{8,9},{9,10},{10,11},{12,13},{... | collective-permute-start | bytes 1179656 | tf_op jit(solution)/shard_map/ppermute | solution.py:283
  22.5 11.4 %collective-permute-start.3 = (f32[768,128]{1,0:T(8,128)}, f32[768,128]{1,0:T(8,128)S(1)}, u32[]{:S(2)}, u32[]{:S(2)}) collective-permute-start(f32[768,128]{1,0:T(8,128)} %get-tuple-element.18), channel_id=1, source_target_pairs={{1,0},{2,1},{3,2},{5,4},{6,5},{7,6},{9,8},{10,9},{11,10},{13,12},{... | collective-permute-start | bytes 1179656 | tf_op jit(solution)/shard_map/ppermute | solution.py:284
  54.0 22.5 %all-to-all-start.2 = ((f32[16,32,128]{2,1,0:T(8,128)}), f32[16,32,128]{2,1,0:T(8,128)S(1)}, u32[]{:S(2)}, u32[]{:S(2)}) async-start(f32[16,32,128]{2,1,0:T(8,128)} %coarse_mid.1), calls=%async_computation.2 | async-start | bytes 524288 | tf_op jit(solution)/shard_map/all_to_all | solution.py:269
  94.0 10.9 %all-to-all-start.4 = ((f32[16,16,128]{2,1,0:T(8,128)}), f32[16,16,128]{2,1,0:T(8,128)S(1)}, u32[]{:S(2)}, u32[]{:S(2)}) async-start(f32[16,16,128]{2,1,0:T(8,128)} %coarse_sol.1), calls=%async_computation.4 | async-start | bytes 262144 | tf_op jit(solution)/shard_map/all_to_all | solution.py:269

commit v2 on v1

v2 whole, which is shorter than its diff:
```python
import jax
import jax.numpy as jnp
from jax import lax
from jax.experimental import pallas as pl
from jax.experimental.pallas import tpu as pltpu
from jax.sharding import Mesh
from jax.sharding import PartitionSpec as P

SUB = ("z", "y", "core")
ROWS = ("y", "x")
COLS = ("z", "core")
exact = lax.Precision.HIGHEST

K = 32
F = 48
LANES = 128


def dot(a, b, dims=((1,), (0,))):
    return lax.dot_general(a, b, (dims, ((), ())), precision=exact, preferred_element_type=jnp.float32)


def halves(a):
    high = a.astype(jnp.bfloat16)
    return high, (a - high.astype(jnp.float32)).astype(jnp.bfloat16)


def dot3(a, b, dims=((1,), (0,))):
    a_high, a_low = halves(a)
    b_high, b_low = halves(b)

    def part(u, v):
        return lax.dot_general(u, v, (dims, ((), ())), preferred_element_type=jnp.float32)

    return part(a_high, b_high) + (part(a_high, b_low) + part(a_low, b_high))


def line(ref, f):
    return ref[pl.ds(f, K, stride=F), :]


def place(c, x, y):
    return (c * 4 + x) * 4 + y


def wide(ref):
    return jnp.concatenate([line(ref, f) for f in range(F)], axis=1)


def narrow(value, ref):
    for f in range(F):
        ref[pl.ds(f, K, stride=F), :] = value[:, f * LANES : (f + 1) * LANES]


def call(kernel, outs, fetched, stored, scratch=(), flops=10_000_000, unread=0, name=None, held=0):
    def run(*args):
        n, m = len(args), len(outs)
        whole = n - unread - fetched
        vmem, hbm = pl.BlockSpec(memory_space=pltpu.VMEM), pl.BlockSpec(memory_space=pltpu.HBM)

        def body(*refs):
            given, made, own = refs[:n], refs[n : n + m], refs[n + m :]
            buffers, semaphores = own[: fetched + stored], own[fetched + stored : 2 * (fetched + stored)]
            rest = own[2 * (fetched + stored) :]
            fetches = [
                pltpu.make_async_copy(*three) for three in zip(given[:fetched], buffers[:fetched], semaphores[:fetched])
            ]
            stores = [
                pltpu.make_async_copy(*three) for three in zip(buffers[fetched:], made[:stored], semaphores[fetched:])
            ]
            for fetch in fetches:
                fetch.start()
            kernel(
                lambda i: fetches[i].wait(),
                lambda i: stores[i].start(),
                *buffers[:fetched],
                *given[fetched : fetched + whole],
                *buffers[fetched:],
                *made[stored:],
                *rest,
            )
            for store in stores:
                store.wait()

        sizes = [a.size for a in args[: fetched + whole]]
        for o in outs:
            sizes.append(1)
            for length in o:
                sizes[-1] *= length
        return pl.pallas_call(
            body,
            out_shape=[pltpu.HBM(o, jnp.float32) for o in outs[:stored]]
            + [jax.ShapeDtypeStruct(o, jnp.float32) for o in outs[stored:]],
            in_specs=[hbm] * fetched + [vmem] * whole + [hbm] * unread,
            out_specs=[hbm] * stored + [vmem] * (m - stored),
            scratch_shapes=[pltpu.VMEM(a.shape, jnp.float32) for a in args[:fetched]]
            + [pltpu.VMEM(o, jnp.float32) for o in outs[:stored]]
            + [pltpu.SemaphoreType.DMA] * (fetched + stored)
            + [pltpu.VMEM(shape, jnp.float32) for shape in scratch],
            compiler_params=pltpu.CompilerParams(vmem_limit_bytes=24 * 1024 * 1024),
            cost_estimate=pl.CostEstimate(flops=flops, bytes_accessed=4 * sum(sizes), transcendentals=0),
            name=name,
            )(
            *(pltpu.with_memory_space_constraint(a, pltpu.HBM) for a in args[:fetched]),
            *(pltpu.with_memory_space_constraint(a, pltpu.VMEM) for a in args[fetched : fetched + held]),
            *args[fetched + held :],
        )

    return run


def slab_kernel(p_hbm, factor, low_x, high_x, low_y, high_y, blocks, p, whole, fetched, sent):
    fetch = pltpu.make_async_copy(p_hbm, p, fetched.at[0])
    fetch.start()
    other = pltpu.make_async_copy(factor, whole, fetched.at[1])
    other.start()
    cuts = [
        pltpu.make_async_copy(whole.at[:, pl.ds(g * 512, 512)], blocks.at[g], sent.at[g]) for g in range(16)
    ]
    fetch.wait()
    other.wait()
    for cut in cuts:
        cut.start()
    at = 0
    for c in range(3):
        for x in range(2):
            for y in range(4):
                low_x[pl.ds(at * K, K), :] = line(p, place(c, x, y))
                high_x[pl.ds(at * K, K), :] = line(p, place(c, x + 2, y))
                at += 1
    at = 0
    for c in range(3):
        for x in range(4):
            for y in range(2):
                low_y[pl.ds(at * K, K), :] = line(p, place(c, x, y))
                high_y[pl.ds(at * K, K), :] = line(p, place(c, x, y + 2))
                at += 1
    for cut in cuts:
        cut.wait()


def halo_slabs(p, factor):
    rows = p.shape[0]
    hbm, vmem = pl.BlockSpec(memory_space=pltpu.HBM), pl.BlockSpec(memory_space=pltpu.VMEM)
    return pl.pallas_call(
        slab_kernel,
        out_shape=[jax.ShapeDtypeStruct((rows // 2, LANES), jnp.float32)] * 4 + [pltpu.HBM((16, K, 512), jnp.float32)],
        in_specs=[hbm] * 2,
        out_specs=[vmem] * 4 + [hbm],
        scratch_shapes=[
            pltpu.VMEM(p.shape, jnp.float32),
            pltpu.VMEM(factor.shape, jnp.float32),
            pltpu.SemaphoreType.DMA((2,)),
            pltpu.SemaphoreType.DMA((16,)),
        ],
        compiler_params=pltpu.CompilerParams(vmem_limit_bytes=24 * 1024 * 1024),
        cost_estimate=pl.CostEstimate(flops=1_000_000, bytes_accessed=5_000_000, transcendentals=0),
        name="halo_slabs",
    )(*(pltpu.with_memory_space_constraint(a, pltpu.HBM) for a in (p, factor)))


def image_kernel(wait, put, p, mass, inverse, basis, r, below_y, above_y, below_x, above_x, q, sums, inner, left, right, lines):
    lane = lax.broadcasted_iota(jnp.int32, (K, LANES), 1)

    def at(c, x, y):
        if x < 0:
            return below_x[pl.ds(((c * 2 + x + 2) * 4 + y) * K, K), :]
        if x > 3:
            return above_x[pl.ds(((c * 2 + x - 4) * 4 + y) * K, K), :]
        if y < 0:
            return below_y[pl.ds(((c * 4 + x) * 2 + y + 2) * K, K), :]
        if y > 3:
            return above_y[pl.ds(((c * 4 + x) * 2 + y - 4) * K, K), :]
        return left[pl.ds(0, K), pl.ds(place(c, x, y) * LANES, LANES)]

    wait(0)
    for f in range(F):
        left[pl.ds(0, K), pl.ds(f * LANES, LANES)] = line(p, f)
    wait(1)
    for c in range(3):
        for x in range(4):
            for y in range(4):
                f = place(c, x, y)
                center = at(c, x, y)
                near = at(c, x - 1, y) + at(c, x + 1, y) + at(c, x, y - 1) + at(c, x, y + 1)
                far = at(c, x - 2, y) + at(c, x + 2, y) + at(c, x, y - 2) + at(c, x, y + 2)
                near = near + jnp.where(lane >= 1, pltpu.roll(center, 1, 1), 0.0)
                near = near + jnp.where(lane < LANES - 1, pltpu.roll(center, LANES - 1, 1), 0.0)
                far = far + jnp.where(lane >= 2, pltpu.roll(center, 2, 1), 0.0)
                far = far + jnp.where(lane < LANES - 2, pltpu.roll(center, LANES - 2, 1), 0.0)
                weight = mass[pl.ds(x * 4 + y, 1), :] + 7.5
                value = weight * center - (4.0 / 3.0) * near + (1.0 / 12.0) * far
                q[:, pl.ds(f * LANES, LANES)] = value
                right[pl.ds(0, K), pl.ds(f * LANES, LANES)] = value
                lines[pl.ds(f * K, K), :] = value
    put(0)
    wait(2)
    lines[...] = dot3(lines[...], inverse[...])
    wait(3)
    wait(4)
    for f in range(F):
        columns = pl.ds(f * LANES, LANES)
        left[pl.ds(K, K), columns] = line(basis, f)
        left[pl.ds(2 * K, K), columns] = lines[pl.ds(f * K, K), :]
        right[pl.ds(K, K), columns] = line(r, f)
    every = dot3(left[...], right[...], ((1,), (1,)))
    sums[...] = jnp.concatenate([every[:K], every[K : 2 * K]], axis=1)
    inner[...] = every[2 * K :]


def slots(axis):
    own = lax.axis_index(axis)
    return [lax.rem(own + 4 - d, 4) for d in range(4)]


def gather_y_kernel(wait, put, sums_0, sums_1, sums_2, sums_3, out, lines):
    total = jnp.zeros((K, 64), jnp.float32)
    for slot, arrived in zip(slots("y"), (sums_0, sums_1, sums_2, sums_3)):
        lines[pl.ds(pl.multiple_of(slot * K, K), K), :] = arrived[...]
        total = total + arrived[:, :64]
    out[pl.ds(0, 64), :] = jnp.concatenate([lines[pl.ds(0, 64), :][:, 64:], lines[pl.ds(64, 64), :][:, 64:]], axis=1)
    out[pl.ds(64, 16), :] = jnp.concatenate([total[:16], total[16:]], axis=1)


def mid_kernel(wait, put, factor, group_0, group_1, group_2, group_3, out, rhs):
    total = jnp.zeros((16, LANES), jnp.float32)
    for slot, arrived in zip(slots("x"), (group_0, group_1, group_2, group_3)):
        for y in range(4):
            piece = arrived[pl.ds((y % 2) * K, K), :][:, (y // 2) * 64 : (y // 2 + 1) * 64]
            rhs[pl.ds(pl.multiple_of((y * 4 + slot) * K, K), K), :] = piece
        total = total + arrived[pl.ds(64, 16), :]
    total = jnp.concatenate([total[:, :64], total[:, 64:]], axis=0)
    mid = dot3(rhs[...].T, factor[...].reshape(512, 512)).T
    for g in range(16):
        out[g] = jnp.concatenate([mid[g * K : (g + 1) * K], total], axis=1)


def packed4(a, b):
    return jnp.concatenate([a[:16], a[16:], b[:16], b[16:]], axis=1)


def alpha_kernel(wait, put, arrived, inner, alpha, gram_inverse, out):
    total = jnp.sum(arrived[...], axis=0)
    mid_q, mid_r = total[:, :32], total[:, 32:64]
    gram, proj = total[:, 64:96], total[:, 96:]
    row = lax.broadcasted_iota(jnp.int32, (K, K), 0)
    column = lax.broadcasted_iota(jnp.int32, (K, K), 1)
    work = jnp.concatenate([gram, (row == column).astype(jnp.float32), proj], axis=1)
    at = lax.broadcasted_iota(jnp.int32, (K, 1), 0)
    for j in range(0, K, 2):
        first, second = work[j : j + 1, :], work[j + 1 : j + 2, :]
        pivot = 1.0 / first[:, j : j + 1]
        scaled = first * pivot
        second = second - second[:, j : j + 1] * scaled
        second = second * (1.0 / second[:, j + 1 : j + 2])
        first = scaled - scaled[:, j + 1 : j + 2] * second
        rest = work - work[:, j : j + 1] * first - work[:, j + 1 : j + 2] * second
        work = jnp.where(at == j, first, jnp.where(at == j + 1, second, rest))
    mix = work[:, 2 * K :]
    inverse = work[:, K : 2 * K]
    alpha[...] = mix
    gram_inverse[...] = inverse
    coarse_mid = mid_r - dot(mid_q, mix)
    cross = inner[:, K:] - dot(inner[:, :K], mix) + dot(mid_q, coarse_mid, ((0,), (0,)))
    packed = packed4(coarse_mid, cross)
    for g in range(16):
        out[g] = packed


def sol_kernel(wait, put, factor, gathered, out):
    cross = jnp.sum(gathered[...], axis=0)[:, 64:]
    mid = jnp.concatenate([gathered[g][:, h : h + K] for g in range(16) for h in (0, K)], axis=0)
    sol = dot3(factor[...].reshape(512, 512), mid)
    for g in range(16):
        at = g * K
        out[g] = jnp.concatenate([sol[at : at + 16], sol[at + 16 : at + K], cross], axis=1)


def update_kernel(wait, put, q, r, inverse, s, p, basis, alpha, new_s, new_r, local, left, lines):
    mix = alpha[...]
    wait(0)
    wait(1)
    narrow(wide(r) - dot3(mix, q[...], ((0,), (0,))), new_r)
    put(1)
    wait(2)
    lines[...] = dot3(new_r[...], inverse[...], ((1,), (1,)))
    local[...] = wide(lines)
    wait(3)
    wait(4)
    wait(5)
    for f in range(F):
        columns = pl.ds(f * LANES, LANES)
        left[pl.ds(0, K), columns] = line(p, f)
        left[pl.ds(K, K), columns] = line(basis, f)
    narrow(wide(s) + dot3(mix, left[pl.ds(0, K), :], ((0,), (0,))), new_s)
    put(0)


def direction_kernel(wait, put, left, local, arrived, gram_inverse, new_p):
    total = jnp.sum(arrived[...], axis=0)
    sol = jnp.concatenate([total[:, :32], total[:, 32:64]], axis=0)
    cross = jnp.concatenate([total[:, 64:96], total[:, 96:]], axis=0)
    beta = -dot(gram_inverse[...], cross)
    mix = jnp.concatenate([beta, sol], axis=0)
    narrow(local[...] + dot3(mix, left[...], ((0,), (0,))), new_p)
    put(0)


def swapped(array, axes):
    return lax.all_to_all(array, axes, 0, 0, tiled=True)


def from_all(array, axis):
    n = lax.axis_size(axis)
    return [array] + [lax.ppermute(array, axis, [(i, (i + d) % n) for i in range(n)]) for d in range(1, n)]


def on_device(solution, residual, direction, mass, coarse_basis, line_inverse, coarse_factor):
    shape = direction.shape
    s, r, p, basis = (a.reshape(-1, LANES) for a in (solution, residual, direction, coarse_basis))
    inverse = line_inverse[0, 0]
    rows, length = p.shape
    flat = (K, F * LANES)

    double = (2 * K, F * LANES)
    low_x, high_x, low_y, high_y, blocks = halo_slabs(p, coarse_factor)
    up_sub = [(i, i + 1) for i in range(63)]
    up_inner = [(i, i + 1) for i in range(3)]
    below_y = lax.ppermute(high_y, "x", up_inner)
    above_y = lax.ppermute(low_y, "x", [(b, a) for a, b in up_inner])
    below_x = lax.ppermute(high_x, SUB, up_sub)
    above_x = lax.ppermute(low_x, SUB, [(b, a) for a, b in up_sub])

    factor = swapped(blocks, ROWS)
    q, sums, inner = call(
        image_kernel,
        [flat, (K, LANES), (K, 2 * K)],
        5,
        1,
        [(3 * K, F * LANES), double, (rows, LANES)],
        50_000_000_000,
        held=4,
        name="image",
    )(p, mass.reshape(16, LANES), inverse, basis, r, below_y, above_y, below_x, above_x)
    (group,) = call(gather_y_kernel, [(80, LANES)], 0, 0, [(4 * K, LANES)], name="gather_y")(*from_all(sums, "y"))
    (parts,) = call(mid_kernel, [(16, K, LANES)], 0, 0, [(512, 64)], held=1, name="coarse_mid")(
        factor, *from_all(group, "x")
    )
    arrived = swapped(parts, COLS)
    alpha, gram_inverse, spread = call(alpha_kernel, [(K, K), (K, K), (16, 16, LANES)], 0, 0, name="alpha")(
        arrived, inner
    )
    mids = swapped(spread, COLS)
    new_s, new_r, local, both = call(
        update_kernel, [(rows, LANES)] * 2 + [flat, double], 6, 2, [(rows, LANES)], 75_000_000, name="updates"
    )(q, r, inverse, s, p, basis, alpha)
    (sols,) = call(sol_kernel, [(16, 16, LANES)], 0, 0, held=1, name="coarse_sol")(factor, mids)
    last = swapped(sols, ROWS)
    (new_p,) = call(direction_kernel, [(rows, LANES)], 0, 1, flops=25_000_000, held=2, name="new_direction")(
        both, local, last, gram_inverse
    )
    return new_s.reshape(shape), new_r.reshape(shape), new_p.reshape(shape)


def solution(mesh):
    torus = Mesh(mesh.devices.reshape(8, 4, 2, 4), ("z", "y", "core", "x"))
    field = P(None, None, SUB, "x", None)
    return jax.shard_map(
        on_device,
        mesh=torus,
        in_specs=(field, field, field, P(SUB, "x", None), field, P(SUB, "x", None, None), P(SUB + ("x",), None)),
        out_specs=(field, field, field),
        check_vma=False,
    )
```

time: 110 us -> 99.8 us (0.907)
  Pallas kernels: 33.5 us -> 21.9 us
  blocking collectives: 26.5 us -> 33.8 us
  waiting for transfers between devices: 13.3 us -> 9.69 us
  local copies, waits for them, and re-layouts: 2.29 us -> 0 us
    pallas_call x9 -> x7, Pallas kernels: 33.5 us -> 18.4 us  [run(): pl.pallas_call(body, out_shape=[pltpu.HBM(o, jnp.float32) for o in outs[:...]
    all_to_all x3 -> x2, starting transfers between devices: 21.8 us -> 11.7 us  [swapped(): return lax.all_to_all(array, axes, 0, 0, tiled=True)]
    ppermute x0 -> x6, starting transfers between devices: none -> 10.1 us  [from_all(): lax.ppermute(array, axis, [(i, (i + d) % n) for i in range(n)])]
    ppermute x0 -> x6, waiting for transfers between devices: none -> 7.64 us  [from_all(): lax.ppermute(array, axis, [(i, (i + d) % n) for i in range(n)])]
    all_to_all x2, blocking collectives: 26.5 us -> 33.8 us  [swapped(): return lax.all_to_all(array, axes, 0, 0, tiled=True)]
    all_to_all x3 -> x2, waiting for transfers between devices: 6.56 us -> 2.04 us  [swapped(): return lax.all_to_all(array, axes, 0, 0, tiled=True)]
    pallas_call x0 -> x1, Pallas kernels: none -> 3.49 us  [halo_slabs(): pl.pallas_call(slab_kernel, out_shape=[jax.ShapeDtypeStruct((rows // 2, L...]
    ppermute x1, waiting for transfers between devices: 2.98 us -> 0.01 us  [on_device(): above_y = lax.ppermute(low_y, 'x', [(b, a) for a, b in up_inner])]
  transfers between devices with their start and end apart: 7 -> 12, of which waited for: 5 -> 6; matrix products, arithmetic and copies ran while one was open for 0% -> 0% of each run, Pallas kernels for 17% -> 11%
where the time goes in v2:
time: 99.8 us; the launch traced here: 99.3 us
  blocking collectives  33.8 us (34%)
  starting transfers between devices  33 us (33%)
  Pallas kernels  21.9 us (22%)
  waiting for transfers between devices  9.69 us (10%)
    all_to_all x2, blocking collectives, swapped(): return lax.all_to_all(array, axes, 0, 0, tiled=True)  33.8 us
    pallas_call x7, Pallas kernels, run(): pl.pallas_call(body, out_shape=[pltpu.HBM(o, jnp.float32) for o in outs[:...  18.4 us
    all_to_all x2, starting transfers between devices, swapped(): return lax.all_to_all(array, axes, 0, 0, tiled=True)  11.7 us
    ppermute x6, starting transfers between devices, from_all(): lax.ppermute(array, axis, [(i, (i + d) % n) for i in range(n)])  10.1 us
    ppermute x6, waiting for transfers between devices, from_all(): lax.ppermute(array, axis, [(i, (i + d) % n) for i in range(n)])  7.64 us
    ppermute x1, starting transfers between devices, on_device(): below_x = lax.ppermute(high_x, SUB, up_sub)  4.05 us
    ppermute x1, starting transfers between devices, on_device(): below_y = lax.ppermute(high_y, 'x', up_inner)  3.97 us
    pallas_call x1, Pallas kernels, halo_slabs(): pl.pallas_call(slab_kernel, out_shape=[jax.ShapeDtypeStruct((rows // 2, L...  3.49 us
  transfers between devices with their start and end apart: 12, of which 6 were waited for; matrix products, arithmetic and copies ran while one was open for 0% of the time, Pallas kernels for 11%

profile of v2, /device:TPU:1, one launch (start us, length us, event | category | flops | bytes accessed | tf_op | source)
XLA Modules:
  0.0 99.3 jit_solution(4239685404989905393)
XLA Ops:
  0.6 3.5 %halo_slabs.1 = (f32[768,128]{1,0:T(8,128)S(1)}, f32[768,128]{1,0:T(8,128)S(1)}, f32[768,128]{1,0:T(8,128)}, f32[768,128]{1,0:T(8,128)}, f32[16,32,512]{2,1,0:T(8,128)}) custom-call(f32[1536,128]{1,0:T(8,128)} %bitcast.9, f32[32,8192]{1,0:T(8,128)} %factor.1), custom_call_target="tpu_custom_call" | custom-call | flops 1000000 | bytes 5000000 | tf_op jit(solution)/shard_map/halo_slabs/pallas_call | solution.py:145
  4.1 4.0 %collective-permute-start = (f32[768,128]{1,0:T(8,128)}, f32[768,128]{1,0:T(8,128)S(1)}, u32[]{:S(2)}, u32[]{:S(2)}) collective-permute-start(f32[768,128]{1,0:T(8,128)} %get-tuple-element.18), channel_id=1, source_target_pairs={{0,1},{1,2},{2,3},{4,5},{5,6},{6,7},{8,9},{9,10},{10,11},{12,13},{... | collective-permute-start | bytes 1179656 | tf_op jit(solution)/shard_map/ppermute | solution.py:329
  8.1 1.3 %collective-permute-start.1 = (f32[768,128]{1,0:T(8,128)}, f32[768,128]{1,0:T(8,128)S(1)}, u32[]{:S(2)}, u32[]{:S(2)}) collective-permute-start(f32[768,128]{1,0:T(8,128)} %get-tuple-element.19), channel_id=1, source_target_pairs={{1,0},{2,1},{3,2},{5,4},{6,5},{7,6},{9,8},{10,9},{11,10},{13,12},{... | collective-permute-start | bytes 1179656 | tf_op jit(solution)/shard_map/ppermute | solution.py:330
  9.4 4.0 %collective-permute-start.2 = (f32[768,128]{1,0:T(8,128)S(1)}, f32[768,128]{1,0:T(8,128)S(1)}, u32[]{:S(2)}, u32[]{:S(2)}) collective-permute-start(f32[768,128]{1,0:T(8,128)S(1)} %get-tuple-element.20), channel_id=1, source_target_pairs={{0,4},{4,8},{8,12},{12,16},{16,20},{20,24},{24,28},{28,32},{32,36}... | collective-permute-start | bytes 1179656 | tf_op jit(solution)/shard_map/ppermute | solution.py:331
  13.5 1.9 %collective-permute-start.3 = (f32[768,128]{1,0:T(8,128)S(1)}, f32[768,128]{1,0:T(8,128)}, u32[]{:S(2)}, u32[]{:S(2)}) collective-permute-start(f32[768,128]{1,0:T(8,128)S(1)} %get-tuple-element.21), channel_id=1, source_target_pairs={{4,0},{8,4},{12,8},{16,12},{20,16},{24,20},{28,24},{32,28},{36,32}... | collective-permute-start | bytes 1179656 | tf_op jit(solution)/shard_map/ppermute | solution.py:332
  15.4 7.7 %all-to-all-start = ((f32[16,32,512]{2,1,0:T(8,128)}), f32[16,32,512]{2,1,0:T(8,128)S(1)}, u32[]{:S(2)}, u32[]{:S(2)}) async-start(f32[16,32,512]{2,1,0:T(8,128)} %get-tuple-element.23), calls=%async_computation | async-start | bytes 2097152 | tf_op jit(solution)/shard_map/all_to_all | solution.py:310
  23.1 5.5 %image.1 = (f32[32,6144]{1,0:T(8,128)}, f32[32,128]{1,0:T(8,128)S(1)}, f32[32,64]{1,0:T(8,128)S(1)}) custom-call(f32[1536,128]{1,0:T(8,128)} %bitcast.10, f32[16,128]{1,0:T(8,128)} %bitcast.22, f32[128,128]{1,0:T(8,128)} %bitcast.18, f32[1536,128]{1,0:T(8,128)} %bitcast.13, f32[1536,128]{1,0:T(8,128)} %bitcast.15, ...), custom_call_target="tpu_custom_call" | custom-call | flops 49999998976 | bytes 4816896 | tf_op jit(solution)/shard_map/image/pallas_call | solution.py:90
  28.7 4.5 %collective-permute-start.6 = (f32[32,128]{1,0:T(8,128)S(1)}, f32[32,128]{1,0:T(8,128)S(1)}, u32[]{:S(2)}, u32[]{:S(2)}) collective-permute-start(f32[32,128]{1,0:T(8,128)S(1)} %get-tuple-element.24.refs_0_), channel_id=1, source_target_pairs={{0,24},{8,0},{16,8},{24,16},{1,25},{9,1},{17,9},{25,17},{2,26},{10... | collective-permute-start | bytes 49160 | tf_op jit(solution)/shard_map/ppermute | solution.py:315
  33.1 0.7 collective-permute-start.4
  33.8 3.2 %collective-permute-done.6.refs_3_ = f32[32,128]{1,0:T(8,128)S(1)} collective-permute-done((f32[32,128]{1,0:T(8,128)S(1)}, f32[32,128]{1,0:T(8,128)S(1)}, u32[]{:S(2)}, u32[]{:S(2)}) %collective-permute-start.6) | collective-permute-done | bytes 16416 | tf_op jit(solution)/shard_map/ppermute | solution.py:315
  37.3 0.5 collective-permute-done.4.refs_1_
  37.9 3.7 %collective-permute-start.9 = (f32[80,128]{1,0:T(8,128)S(1)}, f32[80,128]{1,0:T(8,128)S(1)}, u32[]{:S(2)}, u32[]{:S(2)}) collective-permute-start(f32[80,128]{1,0:T(8,128)S(1)} %gather_y.1.refs_1_), channel_id=1, source_target_pairs={{0,3},{1,0},{2,1},{3,2},{4,7},{5,4},{6,5},{7,6},{8,11},{9,8},{10,9... | collective-permute-start | bytes 122888 | tf_op jit(solution)/shard_map/ppermute | solution.py:315
  41.6 0.8 collective-permute-start.8
  42.8 3.2 %collective-permute-done.8.refs_3_ = f32[80,128]{1,0:T(8,128)S(1)} collective-permute-done((f32[80,128]{1,0:T(8,128)S(1)}, f32[80,128]{1,0:T(8,128)S(1)}, u32[]{:S(2)}, u32[]{:S(2)}) %collective-permute-start.8) | collective-permute-done | bytes 40992 | tf_op jit(solution)/shard_map/ppermute | solution.py:315
  46.0 0.5 collective-permute-done.7.refs_2_
  46.5 0.7 coarse_mid.1
  47.2 21.9 %all_to_all.20.refs_0_ = f32[16,32,128]{2,1,0:T(8,128)S(1)} all-to-all(f32[16,32,128]{2,1,0:T(8,128)S(1)} %coarse_mid.1), channel_id=1, replica_groups=mesh['z'=8,'y'=4,'core'=2,'x'=4] {'z','core'}, dimensions={0} | all-to-all | bytes 524288 | tf_op jit(solution)/shard_map/all_to_all | solution.py:310
  69.1 3.5 %alpha.1 = (f32[32,32]{1,0:T(8,128)S(1)}, f32[32,32]{1,0:T(8,128)S(1)}, f32[16,16,128]{2,1,0:T(8,128)S(1)}) custom-call(f32[16,32,128]{2,1,0:T(8,128)S(1)} %all_to_all.20.refs_0_, f32[32,64]{1,0:T(8,128)S(1)} %get-tuple-element.25.refs_1_), custom_call_target="tpu_custom_call" | custom-call | flops 10000000 | bytes 409600 | tf_op jit(solution)/shard_map/alpha/pallas_call | solution.py:90
  72.6 11.9 %all_to_all.21.refs_1_ = f32[16,16,128]{2,1,0:T(8,128)S(1)} all-to-all(f32[16,16,128]{2,1,0:T(8,128)S(1)} %get-tuple-element.31), channel_id=1, replica_groups=mesh['z'=8,'y'=4,'core'=2,'x'=4] {'z','core'}, dimensions={0} | all-to-all | bytes 262144 | tf_op jit(solution)/shard_map/all_to_all | solution.py:310
  84.4 1.4 %coarse_sol.1 = f32[16,16,128]{2,1,0:T(8,128)} custom-call(f32[16,32,512]{2,1,0:T(8,128)S(1)} %all-to-all-done.refs_0_, f32[16,16,128]{2,1,0:T(8,128)S(1)} %all_to_all.21.refs_1_), custom_call_target="tpu_custom_call" | custom-call | flops 10000000 | bytes 1310720 | tf_op jit(solution)/shard_map/coarse_sol/pallas_call | solution.py:90
  85.8 4.0 %all-to-all-start.3 = ((f32[16,16,128]{2,1,0:T(8,128)}), f32[16,16,128]{2,1,0:T(8,128)S(1)}, u32[]{:S(2)}, u32[]{:S(2)}) async-start(f32[16,16,128]{2,1,0:T(8,128)} %coarse_sol.1), calls=%async_computation.3 | async-start | bytes 262144 | tf_op jit(solution)/shard_map/all_to_all | solution.py:310
  89.8 5.3 %updates.1 = (f32[1536,128]{1,0:T(8,128)}, f32[1536,128]{1,0:T(8,128)}, f32[32,6144]{1,0:T(8,128)S(1)}, f32[64,6144]{1,0:T(8,128)S(1)}) custom-call(f32[32,6144]{1,0:T(8,128)} %get-tuple-element.22.refs_0_, f32[1536,128]{1,0:T(8,128)} %bitcast.16, f32[128,128]{1,0:T(8,128)} %bitcast.19, f32[1536,128]{1,0:T(8,128)} %bitcast.17, f32[1536,128]{1,0:T(8,128)} %bitcast.11, ...), custom_call_target="tpu_custom_call" | custom-call | flops 75000000 | bytes 7933952 | tf_op jit(solution)/shard_map/updates/pallas_call | solution.py:90
  95.2 2.0 %all-to-all-done.3.refs_2_ = f32[16,16,128]{2,1,0:T(8,128)S(1)} async-done(((f32[16,16,128]{2,1,0:T(8,128)}), f32[16,16,128]{2,1,0:T(8,128)S(1)}, u32[]{:S(2)}, u32[]{:S(2)}) %all-to-all-start.3) | async-done | bytes 131104 | tf_op jit(solution)/shard_map/all_to_all | solution.py:310
  97.2 1.9 %new_direction.1 = f32[1536,128]{1,0:T(8,128)} custom-call(f32[64,6144]{1,0:T(8,128)S(1)} %get-tuple-element.29.refs_0_, f32[32,6144]{1,0:T(8,128)S(1)} %get-tuple-element.30.refs_1_, f32[16,16,128]{2,1,0:T(8,128)S(1)} %all-to-all-done.3.refs_2_, f32[32,32]{1,0:T(8,128)S(1)} %get-tuple-element.32.refs_3_), custom_call_target="tpu_custom_call" | custom-call | flops 25000000 | bytes 3280896 | tf_op jit(solution)/shard_map/new_direction/pallas_call | solution.py:90
  (10 shorter events, 0.9 us)
Async XLA Ops:
  4.1 19.0 %collective-permute-start = (f32[768,128]{1,0:T(8,128)}, f32[768,128]{1,0:T(8,128)S(1)}, u32[]{:S(2)}, u32[]{:S(2)}) collective-permute-start(f32[768,128]{1,0:T(8,128)} %get-tuple-element.18), channel_id=1, source_target_pairs={{0,1},{1,2},{2,3},{4,5},{5,6},{6,7},{8,9},{9,10},{10,11},{12,13},{... | collective-permute-start | bytes 1179656 | tf_op jit(solution)/shard_map/ppermute | solution.py:329
  8.1 15.0 %collective-permute-start.1 = (f32[768,128]{1,0:T(8,128)}, f32[768,128]{1,0:T(8,128)S(1)}, u32[]{:S(2)}, u32[]{:S(2)}) collective-permute-start(f32[768,128]{1,0:T(8,128)} %get-tuple-element.19), channel_id=1, source_target_pairs={{1,0},{2,1},{3,2},{5,4},{6,5},{7,6},{9,8},{10,9},{11,10},{13,12},{... | collective-permute-start | bytes 1179656 | tf_op jit(solution)/shard_map/ppermute | solution.py:330
  9.4 13.7 %collective-permute-start.2 = (f32[768,128]{1,0:T(8,128)S(1)}, f32[768,128]{1,0:T(8,128)S(1)}, u32[]{:S(2)}, u32[]{:S(2)}) collective-permute-start(f32[768,128]{1,0:T(8,128)S(1)} %get-tuple-element.20), channel_id=1, source_target_pairs={{0,4},{4,8},{8,12},{12,16},{16,20},{20,24},{24,28},{28,32},{32,36}... | collective-permute-start | bytes 1179656 | tf_op jit(solution)/shard_map/ppermute | solution.py:331
  13.5 9.7 %collective-permute-start.3 = (f32[768,128]{1,0:T(8,128)S(1)}, f32[768,128]{1,0:T(8,128)}, u32[]{:S(2)}, u32[]{:S(2)}) collective-permute-start(f32[768,128]{1,0:T(8,128)S(1)} %get-tuple-element.21), channel_id=1, source_target_pairs={{4,0},{8,4},{12,8},{16,12},{20,16},{24,20},{28,24},{32,28},{36,32}... | collective-permute-start | bytes 1179656 | tf_op jit(solution)/shard_map/ppermute | solution.py:332
  15.4 31.1 %all-to-all-start = ((f32[16,32,512]{2,1,0:T(8,128)}), f32[16,32,512]{2,1,0:T(8,128)S(1)}, u32[]{:S(2)}, u32[]{:S(2)}) async-start(f32[16,32,512]{2,1,0:T(8,128)} %get-tuple-element.23), calls=%async_computation | async-start | bytes 2097152 | tf_op jit(solution)/shard_map/all_to_all | solution.py:310
  28.7 8.3 %collective-permute-start.6 = (f32[32,128]{1,0:T(8,128)S(1)}, f32[32,128]{1,0:T(8,128)S(1)}, u32[]{:S(2)}, u32[]{:S(2)}) collective-permute-start(f32[32,128]{1,0:T(8,128)S(1)} %get-tuple-element.24.refs_0_), channel_id=1, source_target_pairs={{0,24},{8,0},{16,8},{24,16},{1,25},{9,1},{17,9},{25,17},{2,26},{10... | collective-permute-start | bytes 49160 | tf_op jit(solution)/shard_map/ppermute | solution.py:315
  33.1 4.2 %collective-permute-start.5 = (f32[32,128]{1,0:T(8,128)S(1)}, f32[32,128]{1,0:T(8,128)S(1)}, u32[]{:S(2)}, u32[]{:S(2)}) collective-permute-start(f32[32,128]{1,0:T(8,128)S(1)} %get-tuple-element.24.refs_0_), channel_id=1, source_target_pairs={{0,16},{8,24},{16,0},{24,8},{1,17},{9,25},{17,1},{25,9},{2,18},{10... | collective-permute-start | bytes 49160 | tf_op jit(solution)/shard_map/ppermute | solution.py:315
  33.1 4.7 %collective-permute-start.4 = (f32[32,128]{1,0:T(8,128)S(1)}, f32[32,128]{1,0:T(8,128)S(1)}, u32[]{:S(2)}, u32[]{:S(2)}) collective-permute-start(f32[32,128]{1,0:T(8,128)S(1)} %get-tuple-element.24.refs_0_), channel_id=1, source_target_pairs={{0,8},{8,16},{16,24},{24,0},{1,9},{9,17},{17,25},{25,1},{2,10},{10... | collective-permute-start | bytes 49160 | tf_op jit(solution)/shard_map/ppermute | solution.py:315
  37.9 4.9 %collective-permute-start.9 = (f32[80,128]{1,0:T(8,128)S(1)}, f32[80,128]{1,0:T(8,128)S(1)}, u32[]{:S(2)}, u32[]{:S(2)}) collective-permute-start(f32[80,128]{1,0:T(8,128)S(1)} %gather_y.1.refs_1_), channel_id=1, source_target_pairs={{0,3},{1,0},{2,1},{3,2},{4,7},{5,4},{6,5},{7,6},{8,11},{9,8},{10,9... | collective-permute-start | bytes 122888 | tf_op jit(solution)/shard_map/ppermute | solution.py:315
  41.6 4.4 %collective-permute-start.8 = (f32[80,128]{1,0:T(8,128)S(1)}, f32[80,128]{1,0:T(8,128)S(1)}, u32[]{:S(2)}, u32[]{:S(2)}) collective-permute-start(f32[80,128]{1,0:T(8,128)S(1)} %gather_y.1.refs_1_), channel_id=1, source_target_pairs={{0,2},{1,3},{2,0},{3,1},{4,6},{5,7},{6,4},{7,5},{8,10},{9,11},{10,... | collective-permute-start | bytes 122888 | tf_op jit(solution)/shard_map/ppermute | solution.py:315
  42.4 4.1 %collective-permute-start.7 = (f32[80,128]{1,0:T(8,128)S(1)}, f32[80,128]{1,0:T(8,128)S(1)}, u32[]{:S(2)}, u32[]{:S(2)}) collective-permute-start(f32[80,128]{1,0:T(8,128)S(1)} %gather_y.1.refs_1_), channel_id=1, source_target_pairs={{0,1},{1,2},{2,3},{3,0},{4,5},{5,6},{6,7},{7,4},{8,9},{9,10},{10,1... | collective-permute-start | bytes 122888 | tf_op jit(solution)/shard_map/ppermute | solution.py:315
  85.8 11.4 %all-to-all-start.3 = ((f32[16,16,128]{2,1,0:T(8,128)}), f32[16,16,128]{2,1,0:T(8,128)S(1)}, u32[]{:S(2)}, u32[]{:S(2)}) async-start(f32[16,16,128]{2,1,0:T(8,128)} %coarse_sol.1), calls=%async_computation.3 | async-start | bytes 262144 | tf_op jit(solution)/shard_map/all_to_all | solution.py:310

commit v3 on v2

--- a/solution.py
+++ b/solution.py
@@ -8,7 +8,7 @@
 
 SUB = ("z", "y", "core")
 ROWS = ("y", "x")
-COLS = ("z", "core")
+COLS = ("core", "z")
 exact = lax.Precision.HIGHEST
 
 K = 32
@@ -159,7 +159,7 @@
     )(*(pltpu.with_memory_space_constraint(a, pltpu.HBM) for a in (p, factor)))
 
 
-def image_kernel(wait, put, p, mass, inverse, basis, r, below_y, above_y, below_x, above_x, q, sums, inner, left, right, lines):
+def image_kernel(wait, put, p, mass, inverse, basis, r, below_x, below_y, above_y, above_x, q, sums, inner, left, right, lines):
     lane = lax.broadcasted_iota(jnp.int32, (K, LANES), 1)
 
     def at(c, x, y):
@@ -243,6 +243,7 @@
     total = jnp.sum(arrived[...], axis=0)
     mid_q, mid_r = total[:, :32], total[:, 32:64]
     gram, proj = total[:, 64:96], total[:, 96:]
+    base = inner[...] + dot(mid_q, total[:, : 2 * K], ((0,), (0,)))
     row = lax.broadcasted_iota(jnp.int32, (K, K), 0)
     column = lax.broadcasted_iota(jnp.int32, (K, K), 1)
     work = jnp.concatenate([gram, (row == column).astype(jnp.float32), proj], axis=1)
@@ -260,8 +261,9 @@
     inverse = work[:, K : 2 * K]
     alpha[...] = mix
     gram_inverse[...] = inverse
-    coarse_mid = mid_r - dot(mid_q, mix)
-    cross = inner[:, K:] - dot(inner[:, :K], mix) + dot(mid_q, coarse_mid, ((0,), (0,)))
+    after = dot(jnp.concatenate([mid_q, base[:, :K]], axis=0), mix)
+    coarse_mid = mid_r - after[:K]
+    cross = base[:, K:] - after[K:]
     packed = packed4(coarse_mid, cross)
     for g in range(16):
         out[g] = packed
@@ -326,11 +328,11 @@
     low_x, high_x, low_y, high_y, blocks = halo_slabs(p, coarse_factor)
     up_sub = [(i, i + 1) for i in range(63)]
     up_inner = [(i, i + 1) for i in range(3)]
+    below_x = lax.ppermute(high_x, SUB, up_sub)
+    above_x = lax.ppermute(low_x, SUB, [(b, a) for a, b in up_sub])
+
     below_y = lax.ppermute(high_y, "x", up_inner)
     above_y = lax.ppermute(low_y, "x", [(b, a) for a, b in up_inner])
-    below_x = lax.ppermute(high_x, SUB, up_sub)
-    above_x = lax.ppermute(low_x, SUB, [(b, a) for a, b in up_sub])
-
     factor = swapped(blocks, ROWS)
     q, sums, inner = call(
         image_kernel,
@@ -341,7 +343,7 @@
         50_000_000_000,
         held=4,
         name="image",
-    )(p, mass.reshape(16, LANES), inverse, basis, r, below_y, above_y, below_x, above_x)
+    )(p, mass.reshape(16, LANES), inverse, basis, r, below_x, below_y, above_y, above_x)
     (group,) = call(gather_y_kernel, [(80, LANES)], 0, 0, [(4 * K, LANES)], name="gather_y")(*from_all(sums, "y"))
     (parts,) = call(mid_kernel, [(16, K, LANES)], 0, 0, [(512, 64)], held=1, name="coarse_mid")(
         factor, *from_all(group, "x")

time: 99.8 us -> 97.5 us (0.977)
  blocking collectives: 33.8 us -> 31.9 us
  starting transfers between devices: 33 us -> 31.7 us
    all_to_all x2, blocking collectives: 33.8 us -> 31.9 us  [swapped(): return lax.all_to_all(array, axes, 0, 0, tiled=True)]
    ppermute x1, waiting for transfers between devices: 0.01 us -> 1.45 us  [on_device(): above_y = lax.ppermute(low_y, 'x', [(b, a) for a, b in up_inner])]
  transfers between devices with their start and end apart: 12 -> 12, of which waited for: 6 -> 7; matrix products, arithmetic and copies ran while one was open for 0% -> 0% of each run, Pallas kernels for 11% -> 11%
where the time goes in v3:
time: 97.5 us; the launch traced here: 96 us
  blocking collectives  31.9 us (33%)
  starting transfers between devices  31.7 us (33%)
  Pallas kernels  21.6 us (22%)
  waiting for transfers between devices  9.94 us (10%)
    all_to_all x2, blocking collectives, swapped(): return lax.all_to_all(array, axes, 0, 0, tiled=True)  31.9 us
    pallas_call x7, Pallas kernels, run(): pl.pallas_call(body, out_shape=[pltpu.HBM(o, jnp.float32) for o in outs[:...  18.1 us
    all_to_all x2, starting transfers between devices, swapped(): return lax.all_to_all(array, axes, 0, 0, tiled=True)  11.4 us
    ppermute x6, starting transfers between devices, from_all(): lax.ppermute(array, axis, [(i, (i + d) % n) for i in range(n)])  9.29 us
    ppermute x6, waiting for transfers between devices, from_all(): lax.ppermute(array, axis, [(i, (i + d) % n) for i in range(n)])  6.99 us
    ppermute x1, starting transfers between devices, on_device(): below_x = lax.ppermute(high_x, SUB, up_sub)  4.59 us
    pallas_call x1, Pallas kernels, halo_slabs(): pl.pallas_call(slab_kernel, out_shape=[jax.ShapeDtypeStruct((rows // 2, L...  3.49 us
    ppermute x1, starting transfers between devices, on_device(): below_y = lax.ppermute(high_y, 'x', up_inner)  3.14 us
  transfers between devices with their start and end apart: 12, of which 7 were waited for; matrix products, arithmetic and copies ran while one was open for 0% of the time, Pallas kernels for 11%

profile of v3, /device:TPU:1, one launch (start us, length us, event | category | flops | bytes accessed | tf_op | source)
XLA Modules:
  0.0 96.0 jit_solution(946559105639352787)
XLA Ops:
  0.6 3.5 %halo_slabs.1 = (f32[768,128]{1,0:T(8,128)S(1)}, f32[768,128]{1,0:T(8,128)}, f32[768,128]{1,0:T(8,128)S(1)}, f32[768,128]{1,0:T(8,128)}, f32[16,32,512]{2,1,0:T(8,128)}) custom-call(f32[1536,128]{1,0:T(8,128)} %bitcast.9, f32[32,8192]{1,0:T(8,128)} %factor.1), custom_call_target="tpu_custom_call" | custom-call | flops 1000000 | bytes 5000000 | tf_op jit(solution)/shard_map/halo_slabs/pallas_call | solution.py:145
  4.1 4.6 %collective-permute-start = (f32[768,128]{1,0:T(8,128)}, f32[768,128]{1,0:T(8,128)S(1)}, u32[]{:S(2)}, u32[]{:S(2)}) collective-permute-start(f32[768,128]{1,0:T(8,128)} %get-tuple-element.18), channel_id=1, source_target_pairs={{0,4},{4,8},{8,12},{12,16},{16,20},{20,24},{24,28},{28,32},{32,36}... | collective-permute-start | bytes 1179656 | tf_op jit(solution)/shard_map/ppermute | solution.py:331
  8.7 3.1 %collective-permute-start.1 = (f32[768,128]{1,0:T(8,128)}, f32[768,128]{1,0:T(8,128)S(1)}, u32[]{:S(2)}, u32[]{:S(2)}) collective-permute-start(f32[768,128]{1,0:T(8,128)} %get-tuple-element.19), channel_id=1, source_target_pairs={{0,1},{1,2},{2,3},{4,5},{5,6},{6,7},{8,9},{9,10},{10,11},{12,13},{... | collective-permute-start | bytes 1179656 | tf_op jit(solution)/shard_map/ppermute | solution.py:334
  11.9 1.3 %collective-permute-start.2 = (f32[768,128]{1,0:T(8,128)S(1)}, f32[768,128]{1,0:T(8,128)S(1)}, u32[]{:S(2)}, u32[]{:S(2)}) collective-permute-start(f32[768,128]{1,0:T(8,128)S(1)} %get-tuple-element.20), channel_id=1, source_target_pairs={{1,0},{2,1},{3,2},{5,4},{6,5},{7,6},{9,8},{10,9},{11,10},{13,12},{... | collective-permute-start | bytes 1179656 | tf_op jit(solution)/shard_map/ppermute | solution.py:335
  13.2 1.9 %collective-permute-start.3 = (f32[768,128]{1,0:T(8,128)S(1)}, f32[768,128]{1,0:T(8,128)}, u32[]{:S(2)}, u32[]{:S(2)}) collective-permute-start(f32[768,128]{1,0:T(8,128)S(1)} %get-tuple-element.21), channel_id=1, source_target_pairs={{4,0},{8,4},{12,8},{16,12},{20,16},{24,20},{28,24},{32,28},{36,32}... | collective-permute-start | bytes 1179656 | tf_op jit(solution)/shard_map/ppermute | solution.py:332
  15.1 7.4 %all-to-all-start = ((f32[16,32,512]{2,1,0:T(8,128)}), f32[16,32,512]{2,1,0:T(8,128)S(1)}, u32[]{:S(2)}, u32[]{:S(2)}) async-start(f32[16,32,512]{2,1,0:T(8,128)} %get-tuple-element.23), calls=%async_computation | async-start | bytes 2097152 | tf_op jit(solution)/shard_map/all_to_all | solution.py:312
  22.6 1.5 %collective-permute-done.2.refs_7_ = f32[768,128]{1,0:T(8,128)S(1)} collective-permute-done((f32[768,128]{1,0:T(8,128)S(1)}, f32[768,128]{1,0:T(8,128)S(1)}, u32[]{:S(2)}, u32[]{:S(2)}) %collective-permute-start.2) | collective-permute-done | bytes 393248 | tf_op jit(solution)/shard_map/ppermute | solution.py:335
  24.0 5.5 %image.1 = (f32[32,6144]{1,0:T(8,128)}, f32[32,128]{1,0:T(8,128)S(1)}, f32[32,64]{1,0:T(8,128)S(1)}) custom-call(f32[1536,128]{1,0:T(8,128)} %bitcast.10, f32[16,128]{1,0:T(8,128)} %bitcast.22, f32[128,128]{1,0:T(8,128)} %bitcast.18, f32[1536,128]{1,0:T(8,128)} %bitcast.13, f32[1536,128]{1,0:T(8,128)} %bitcast.15, ...), custom_call_target="tpu_custom_call" | custom-call | flops 49999998976 | bytes 4816896 | tf_op jit(solution)/shard_map/image/pallas_call | solution.py:90
  29.5 3.4 %collective-permute-start.6 = (f32[32,128]{1,0:T(8,128)S(1)}, f32[32,128]{1,0:T(8,128)S(1)}, u32[]{:S(2)}, u32[]{:S(2)}) collective-permute-start(f32[32,128]{1,0:T(8,128)S(1)} %get-tuple-element.24.refs_0_), channel_id=1, source_target_pairs={{0,24},{8,0},{16,8},{24,16},{1,25},{9,1},{17,9},{25,17},{2,26},{10... | collective-permute-start | bytes 49160 | tf_op jit(solution)/shard_map/ppermute | solution.py:317
  32.9 0.8 collective-permute-start.4
  33.8 3.2 %collective-permute-done.5.refs_2_ = f32[32,128]{1,0:T(8,128)S(1)} collective-permute-done((f32[32,128]{1,0:T(8,128)S(1)}, f32[32,128]{1,0:T(8,128)S(1)}, u32[]{:S(2)}, u32[]{:S(2)}) %collective-permute-start.5) | collective-permute-done | bytes 16416 | tf_op jit(solution)/shard_map/ppermute | solution.py:317
  37.1 4.0 %collective-permute-start.9 = (f32[80,128]{1,0:T(8,128)S(1)}, f32[80,128]{1,0:T(8,128)S(1)}, u32[]{:S(2)}, u32[]{:S(2)}) collective-permute-start(f32[80,128]{1,0:T(8,128)S(1)} %gather_y.1.refs_1_), channel_id=1, source_target_pairs={{0,3},{1,0},{2,1},{3,2},{4,7},{5,4},{6,5},{7,6},{8,11},{9,8},{10,9... | collective-permute-start | bytes 122888 | tf_op jit(solution)/shard_map/ppermute | solution.py:317
  41.1 0.8 collective-permute-start.8
  42.2 3.2 %collective-permute-done.8.refs_3_ = f32[80,128]{1,0:T(8,128)S(1)} collective-permute-done((f32[80,128]{1,0:T(8,128)S(1)}, f32[80,128]{1,0:T(8,128)S(1)}, u32[]{:S(2)}, u32[]{:S(2)}) %collective-permute-start.8) | collective-permute-done | bytes 40992 | tf_op jit(solution)/shard_map/ppermute | solution.py:317
  45.4 0.5 collective-permute-done.7.refs_2_
  45.9 0.7 coarse_mid.1
  46.6 19.6 %all_to_all.20.refs_0_ = f32[16,32,128]{2,1,0:T(8,128)S(1)} all-to-all(f32[16,32,128]{2,1,0:T(8,128)S(1)} %coarse_mid.1), channel_id=1, replica_groups=mesh['z'=8,'y'=4,'core'=2,'x'=4] {'core','z'}, dimensions={0} | all-to-all | bytes 524288 | tf_op jit(solution)/shard_map/all_to_all | solution.py:312
  66.2 3.2 %alpha.1 = (f32[32,32]{1,0:T(8,128)S(1)}, f32[32,32]{1,0:T(8,128)S(1)}, f32[16,16,128]{2,1,0:T(8,128)S(1)}) custom-call(f32[16,32,128]{2,1,0:T(8,128)S(1)} %all_to_all.20.refs_0_, f32[32,64]{1,0:T(8,128)S(1)} %get-tuple-element.25.refs_1_), custom_call_target="tpu_custom_call" | custom-call | flops 10000000 | bytes 409600 | tf_op jit(solution)/shard_map/alpha/pallas_call | solution.py:90
  69.4 12.3 %all_to_all.21.refs_1_ = f32[16,16,128]{2,1,0:T(8,128)S(1)} all-to-all(f32[16,16,128]{2,1,0:T(8,128)S(1)} %get-tuple-element.31), channel_id=1, replica_groups=mesh['z'=8,'y'=4,'core'=2,'x'=4] {'core','z'}, dimensions={0} | all-to-all | bytes 262144 | tf_op jit(solution)/shard_map/all_to_all | solution.py:312
  81.7 1.4 %coarse_sol.1 = f32[16,16,128]{2,1,0:T(8,128)} custom-call(f32[16,32,512]{2,1,0:T(8,128)S(1)} %all-to-all-done.refs_0_, f32[16,16,128]{2,1,0:T(8,128)S(1)} %all_to_all.21.refs_1_), custom_call_target="tpu_custom_call" | custom-call | flops 10000000 | bytes 1310720 | tf_op jit(solution)/shard_map/coarse_sol/pallas_call | solution.py:90
  83.1 4.0 %all-to-all-start.3 = ((f32[16,16,128]{2,1,0:T(8,128)}), f32[16,16,128]{2,1,0:T(8,128)S(1)}, u32[]{:S(2)}, u32[]{:S(2)}) async-start(f32[16,16,128]{2,1,0:T(8,128)} %coarse_sol.1), calls=%async_computation.3 | async-start | bytes 262144 | tf_op jit(solution)/shard_map/all_to_all | solution.py:312
  87.1 5.3 %updates.1 = (f32[1536,128]{1,0:T(8,128)}, f32[1536,128]{1,0:T(8,128)}, f32[32,6144]{1,0:T(8,128)S(1)}, f32[64,6144]{1,0:T(8,128)S(1)}) custom-call(f32[32,6144]{1,0:T(8,128)} %get-tuple-element.22.refs_0_, f32[1536,128]{1,0:T(8,128)} %bitcast.16, f32[128,128]{1,0:T(8,128)} %bitcast.19, f32[1536,128]{1,0:T(8,128)} %bitcast.17, f32[1536,128]{1,0:T(8,128)} %bitcast.11, ...), custom_call_target="tpu_custom_call" | custom-call | flops 75000000 | bytes 7933952 | tf_op jit(solution)/shard_map/updates/pallas_call | solution.py:90
  92.5 1.5 %all-to-all-done.3.refs_2_ = f32[16,16,128]{2,1,0:T(8,128)S(1)} async-done(((f32[16,16,128]{2,1,0:T(8,128)}), f32[16,16,128]{2,1,0:T(8,128)S(1)}, u32[]{:S(2)}, u32[]{:S(2)}) %all-to-all-start.3) | async-done | bytes 131104 | tf_op jit(solution)/shard_map/all_to_all | solution.py:312
  93.9 1.9 %new_direction.1 = f32[1536,128]{1,0:T(8,128)} custom-call(f32[64,6144]{1,0:T(8,128)S(1)} %get-tuple-element.29.refs_0_, f32[32,6144]{1,0:T(8,128)S(1)} %get-tuple-element.30.refs_1_, f32[16,16,128]{2,1,0:T(8,128)S(1)} %all-to-all-done.3.refs_2_, f32[32,32]{1,0:T(8,128)S(1)} %get-tuple-element.32.refs_3_), custom_call_target="tpu_custom_call" | custom-call | flops 25000000 | bytes 3280896 | tf_op jit(solution)/shard_map/new_direction/pallas_call | solution.py:90
  (10 shorter events, 0.7 us)
Async XLA Ops:
  4.1 18.4 %collective-permute-start = (f32[768,128]{1,0:T(8,128)}, f32[768,128]{1,0:T(8,128)S(1)}, u32[]{:S(2)}, u32[]{:S(2)}) collective-permute-start(f32[768,128]{1,0:T(8,128)} %get-tuple-element.18), channel_id=1, source_target_pairs={{0,4},{4,8},{8,12},{12,16},{16,20},{20,24},{24,28},{28,32},{32,36}... | collective-permute-start | bytes 1179656 | tf_op jit(solution)/shard_map/ppermute | solution.py:331
  8.7 13.8 %collective-permute-start.1 = (f32[768,128]{1,0:T(8,128)}, f32[768,128]{1,0:T(8,128)S(1)}, u32[]{:S(2)}, u32[]{:S(2)}) collective-permute-start(f32[768,128]{1,0:T(8,128)} %get-tuple-element.19), channel_id=1, source_target_pairs={{0,1},{1,2},{2,3},{4,5},{5,6},{6,7},{8,9},{9,10},{10,11},{12,13},{... | collective-permute-start | bytes 1179656 | tf_op jit(solution)/shard_map/ppermute | solution.py:334
  11.9 12.1 %collective-permute-start.2 = (f32[768,128]{1,0:T(8,128)S(1)}, f32[768,128]{1,0:T(8,128)S(1)}, u32[]{:S(2)}, u32[]{:S(2)}) collective-permute-start(f32[768,128]{1,0:T(8,128)S(1)} %get-tuple-element.20), channel_id=1, source_target_pairs={{1,0},{2,1},{3,2},{5,4},{6,5},{7,6},{9,8},{10,9},{11,10},{13,12},{... | collective-permute-start | bytes 1179656 | tf_op jit(solution)/shard_map/ppermute | solution.py:335
  13.2 10.9 %collective-permute-start.3 = (f32[768,128]{1,0:T(8,128)S(1)}, f32[768,128]{1,0:T(8,128)}, u32[]{:S(2)}, u32[]{:S(2)}) collective-permute-start(f32[768,128]{1,0:T(8,128)S(1)} %get-tuple-element.21), channel_id=1, source_target_pairs={{4,0},{8,4},{12,8},{16,12},{20,16},{24,20},{28,24},{32,28},{36,32}... | collective-permute-start | bytes 1179656 | tf_op jit(solution)/shard_map/ppermute | solution.py:332
  15.1 30.8 %all-to-all-start = ((f32[16,32,512]{2,1,0:T(8,128)}), f32[16,32,512]{2,1,0:T(8,128)S(1)}, u32[]{:S(2)}, u32[]{:S(2)}) async-start(f32[16,32,512]{2,1,0:T(8,128)} %get-tuple-element.23), calls=%async_computation | async-start | bytes 2097152 | tf_op jit(solution)/shard_map/all_to_all | solution.py:312
  29.5 4.2 %collective-permute-start.6 = (f32[32,128]{1,0:T(8,128)S(1)}, f32[32,128]{1,0:T(8,128)S(1)}, u32[]{:S(2)}, u32[]{:S(2)}) collective-permute-start(f32[32,128]{1,0:T(8,128)S(1)} %get-tuple-element.24.refs_0_), channel_id=1, source_target_pairs={{0,24},{8,0},{16,8},{24,16},{1,25},{9,1},{17,9},{25,17},{2,26},{10... | collective-permute-start | bytes 49160 | tf_op jit(solution)/shard_map/ppermute | solution.py:317
  32.9 4.1 %collective-permute-start.5 = (f32[32,128]{1,0:T(8,128)S(1)}, f32[32,128]{1,0:T(8,128)S(1)}, u32[]{:S(2)}, u32[]{:S(2)}) collective-permute-start(f32[32,128]{1,0:T(8,128)S(1)} %get-tuple-element.24.refs_0_), channel_id=1, source_target_pairs={{0,16},{8,24},{16,0},{24,8},{1,17},{9,25},{17,1},{25,9},{2,18},{10... | collective-permute-start | bytes 49160 | tf_op jit(solution)/shard_map/ppermute | solution.py:317
  32.9 4.1 %collective-permute-start.4 = (f32[32,128]{1,0:T(8,128)S(1)}, f32[32,128]{1,0:T(8,128)S(1)}, u32[]{:S(2)}, u32[]{:S(2)}) collective-permute-start(f32[32,128]{1,0:T(8,128)S(1)} %get-tuple-element.24.refs_0_), channel_id=1, source_target_pairs={{0,8},{8,16},{16,24},{24,0},{1,9},{9,17},{17,25},{25,1},{2,10},{10... | collective-permute-start | bytes 49160 | tf_op jit(solution)/shard_map/ppermute | solution.py:317
  37.1 5.1 %collective-permute-start.9 = (f32[80,128]{1,0:T(8,128)S(1)}, f32[80,128]{1,0:T(8,128)S(1)}, u32[]{:S(2)}, u32[]{:S(2)}) collective-permute-start(f32[80,128]{1,0:T(8,128)S(1)} %gather_y.1.refs_1_), channel_id=1, source_target_pairs={{0,3},{1,0},{2,1},{3,2},{4,7},{5,4},{6,5},{7,6},{8,11},{9,8},{10,9... | collective-permute-start | bytes 122888 | tf_op jit(solution)/shard_map/ppermute | solution.py:317
  41.1 4.4 %collective-permute-start.8 = (f32[80,128]{1,0:T(8,128)S(1)}, f32[80,128]{1,0:T(8,128)S(1)}, u32[]{:S(2)}, u32[]{:S(2)}) collective-permute-start(f32[80,128]{1,0:T(8,128)S(1)} %gather_y.1.refs_1_), channel_id=1, source_target_pairs={{0,2},{1,3},{2,0},{3,1},{4,6},{5,7},{6,4},{7,5},{8,10},{9,11},{10,... | collective-permute-start | bytes 122888 | tf_op jit(solution)/shard_map/ppermute | solution.py:317
  41.8 4.1 %collective-permute-start.7 = (f32[80,128]{1,0:T(8,128)S(1)}, f32[80,128]{1,0:T(8,128)S(1)}, u32[]{:S(2)}, u32[]{:S(2)}) collective-permute-start(f32[80,128]{1,0:T(8,128)S(1)} %gather_y.1.refs_1_), channel_id=1, source_target_pairs={{0,1},{1,2},{2,3},{3,0},{4,5},{5,6},{6,7},{7,4},{8,9},{9,10},{10,1... | collective-permute-start | bytes 122888 | tf_op jit(solution)/shard_map/ppermute | solution.py:317
  83.1 10.8 %all-to-all-start.3 = ((f32[16,16,128]{2,1,0:T(8,128)}), f32[16,16,128]{2,1,0:T(8,128)S(1)}, u32[]{:S(2)}, u32[]{:S(2)}) async-start(f32[16,16,128]{2,1,0:T(8,128)} %coarse_sol.1), calls=%async_computation.3 | async-start | bytes 262144 | tf_op jit(solution)/shard_map/all_to_all | solution.py:312

commit v4 on v3

--- a/solution.py
+++ b/solution.py
@@ -110,17 +110,24 @@
 
 
 def slab_kernel(p_hbm, factor, low_x, high_x, low_y, high_y, blocks, p, whole, fetched, sent):
-    fetch = pltpu.make_async_copy(p_hbm, p, fetched.at[0])
+    fetch = pltpu.make_async_copy(p_hbm, p, fetched.at[4])
     fetch.start()
-    other = pltpu.make_async_copy(factor, whole, fetched.at[1])
-    other.start()
+    parts = [
+        pltpu.make_async_copy(
+            factor.at[:, pl.ds(i * 2048, 2048)], whole.at[:, pl.ds(i * 2048, 2048)], fetched.at[i]
+        )
+        for i in range(4)
+    ]
+    for part in parts:
+        part.start()
     cuts = [
         pltpu.make_async_copy(whole.at[:, pl.ds(g * 512, 512)], blocks.at[g], sent.at[g]) for g in range(16)
     ]
+    for i, part in enumerate(parts):
+        part.wait()
+        for cut in cuts[4 * i : 4 * i + 4]:
+            cut.start()
     fetch.wait()
-    other.wait()
-    for cut in cuts:
-        cut.start()
     at = 0
     for c in range(3):
         for x in range(2):
@@ -150,7 +157,7 @@
         scratch_shapes=[
             pltpu.VMEM(p.shape, jnp.float32),
             pltpu.VMEM(factor.shape, jnp.float32),
-            pltpu.SemaphoreType.DMA((2,)),
+            pltpu.SemaphoreType.DMA((5,)),
             pltpu.SemaphoreType.DMA((16,)),
         ],
         compiler_params=pltpu.CompilerParams(vmem_limit_bytes=24 * 1024 * 1024),

time: 97.5 us -> 97.2 us (level)
  transfers between devices with their start and end apart: 12 -> 12, of which waited for: 7 -> 6; matrix products, arithmetic and copies ran while one was open for 0% -> 0% of each run, Pallas kernels for 11% -> 11%
where the time goes in v4:
time: 97.2 us; the launch traced here: 95.8 us
  blocking collectives  31.9 us (33%)
  starting transfers between devices  31.7 us (33%)
  Pallas kernels  21.4 us (22%)
  waiting for transfers between devices  9.94 us (10%)
    all_to_all x2, blocking collectives, swapped(): return lax.all_to_all(array, axes, 0, 0, tiled=True)  31.9 us
    pallas_call x7, Pallas kernels, run(): pl.pallas_call(body, out_shape=[pltpu.HBM(o, jnp.float32) for o in outs[:...  18.1 us
    all_to_all x2, starting transfers between devices, swapped(): return lax.all_to_all(array, axes, 0, 0, tiled=True)  11.4 us
    ppermute x6, starting transfers between devices, from_all(): lax.ppermute(array, axis, [(i, (i + d) % n) for i in range(n)])  9.29 us
    ppermute x6, waiting for transfers between devices, from_all(): lax.ppermute(array, axis, [(i, (i + d) % n) for i in range(n)])  6.99 us
    ppermute x1, starting transfers between devices, on_device(): below_x = lax.ppermute(high_x, SUB, up_sub)  4.59 us
    pallas_call x1, Pallas kernels, halo_slabs(): pl.pallas_call(slab_kernel, out_shape=[jax.ShapeDtypeStruct((rows // 2, L...  3.23 us
    ppermute x1, starting transfers between devices, on_device(): below_y = lax.ppermute(high_y, 'x', up_inner)  3.14 us
  transfers between devices with their start and end apart: 12, of which 6 were waited for; matrix products, arithmetic and copies ran while one was open for 0% of the time, Pallas kernels for 11%

profile of v4, /device:TPU:1, one launch (start us, length us, event | category | flops | bytes accessed | tf_op | source)
XLA Modules:
  0.0 95.8 jit_solution(5323830522506355731)
XLA Ops:
  0.6 3.2 %halo_slabs.1 = (f32[768,128]{1,0:T(8,128)S(1)}, f32[768,128]{1,0:T(8,128)}, f32[768,128]{1,0:T(8,128)S(1)}, f32[768,128]{1,0:T(8,128)}, f32[16,32,512]{2,1,0:T(8,128)}) custom-call(f32[1536,128]{1,0:T(8,128)} %bitcast.9, f32[32,8192]{1,0:T(8,128)} %factor.1), custom_call_target="tpu_custom_call" | custom-call | flops 1000000 | bytes 5000000 | tf_op jit(solution)/shard_map/halo_slabs/pallas_call | solution.py:152
  3.9 4.6 %collective-permute-start = (f32[768,128]{1,0:T(8,128)}, f32[768,128]{1,0:T(8,128)S(1)}, u32[]{:S(2)}, u32[]{:S(2)}) collective-permute-start(f32[768,128]{1,0:T(8,128)} %get-tuple-element.18), channel_id=1, source_target_pairs={{0,4},{4,8},{8,12},{12,16},{16,20},{20,24},{24,28},{28,32},{32,36}... | collective-permute-start | bytes 1179656 | tf_op jit(solution)/shard_map/ppermute | solution.py:338
  8.5 3.1 %collective-permute-start.1 = (f32[768,128]{1,0:T(8,128)}, f32[768,128]{1,0:T(8,128)S(1)}, u32[]{:S(2)}, u32[]{:S(2)}) collective-permute-start(f32[768,128]{1,0:T(8,128)} %get-tuple-element.19), channel_id=1, source_target_pairs={{0,1},{1,2},{2,3},{4,5},{5,6},{6,7},{8,9},{9,10},{10,11},{12,13},{... | collective-permute-start | bytes 1179656 | tf_op jit(solution)/shard_map/ppermute | solution.py:341
  11.6 1.3 %collective-permute-start.2 = (f32[768,128]{1,0:T(8,128)S(1)}, f32[768,128]{1,0:T(8,128)S(1)}, u32[]{:S(2)}, u32[]{:S(2)}) collective-permute-start(f32[768,128]{1,0:T(8,128)S(1)} %get-tuple-element.20), channel_id=1, source_target_pairs={{1,0},{2,1},{3,2},{5,4},{6,5},{7,6},{9,8},{10,9},{11,10},{13,12},{... | collective-permute-start | bytes 1179656 | tf_op jit(solution)/shard_map/ppermute | solution.py:342
  12.9 1.9 %collective-permute-start.3 = (f32[768,128]{1,0:T(8,128)S(1)}, f32[768,128]{1,0:T(8,128)}, u32[]{:S(2)}, u32[]{:S(2)}) collective-permute-start(f32[768,128]{1,0:T(8,128)S(1)} %get-tuple-element.21), channel_id=1, source_target_pairs={{4,0},{8,4},{12,8},{16,12},{20,16},{24,20},{28,24},{32,28},{36,32}... | collective-permute-start | bytes 1179656 | tf_op jit(solution)/shard_map/ppermute | solution.py:339
  14.9 7.4 %all-to-all-start = ((f32[16,32,512]{2,1,0:T(8,128)}), f32[16,32,512]{2,1,0:T(8,128)S(1)}, u32[]{:S(2)}, u32[]{:S(2)}) async-start(f32[16,32,512]{2,1,0:T(8,128)} %get-tuple-element.23), calls=%async_computation | async-start | bytes 2097152 | tf_op jit(solution)/shard_map/all_to_all | solution.py:319
  22.3 1.5 %collective-permute-done.2.refs_7_ = f32[768,128]{1,0:T(8,128)S(1)} collective-permute-done((f32[768,128]{1,0:T(8,128)S(1)}, f32[768,128]{1,0:T(8,128)S(1)}, u32[]{:S(2)}, u32[]{:S(2)}) %collective-permute-start.2) | collective-permute-done | bytes 393248 | tf_op jit(solution)/shard_map/ppermute | solution.py:342
  23.8 5.5 %image.1 = (f32[32,6144]{1,0:T(8,128)}, f32[32,128]{1,0:T(8,128)S(1)}, f32[32,64]{1,0:T(8,128)S(1)}) custom-call(f32[1536,128]{1,0:T(8,128)} %bitcast.10, f32[16,128]{1,0:T(8,128)} %bitcast.22, f32[128,128]{1,0:T(8,128)} %bitcast.18, f32[1536,128]{1,0:T(8,128)} %bitcast.13, f32[1536,128]{1,0:T(8,128)} %bitcast.15, ...), custom_call_target="tpu_custom_call" | custom-call | flops 49999998976 | bytes 4816896 | tf_op jit(solution)/shard_map/image/pallas_call | solution.py:90
  29.3 3.4 %collective-permute-start.6 = (f32[32,128]{1,0:T(8,128)S(1)}, f32[32,128]{1,0:T(8,128)S(1)}, u32[]{:S(2)}, u32[]{:S(2)}) collective-permute-start(f32[32,128]{1,0:T(8,128)S(1)} %get-tuple-element.24.refs_0_), channel_id=1, source_target_pairs={{0,24},{8,0},{16,8},{24,16},{1,25},{9,1},{17,9},{25,17},{2,26},{10... | collective-permute-start | bytes 49160 | tf_op jit(solution)/shard_map/ppermute | solution.py:324
  32.7 0.8 collective-permute-start.4
  33.5 3.2 %collective-permute-done.5.refs_2_ = f32[32,128]{1,0:T(8,128)S(1)} collective-permute-done((f32[32,128]{1,0:T(8,128)S(1)}, f32[32,128]{1,0:T(8,128)S(1)}, u32[]{:S(2)}, u32[]{:S(2)}) %collective-permute-start.5) | collective-permute-done | bytes 16416 | tf_op jit(solution)/shard_map/ppermute | solution.py:324
  36.9 4.0 %collective-permute-start.9 = (f32[80,128]{1,0:T(8,128)S(1)}, f32[80,128]{1,0:T(8,128)S(1)}, u32[]{:S(2)}, u32[]{:S(2)}) collective-permute-start(f32[80,128]{1,0:T(8,128)S(1)} %gather_y.1.refs_1_), channel_id=1, source_target_pairs={{0,3},{1,0},{2,1},{3,2},{4,7},{5,4},{6,5},{7,6},{8,11},{9,8},{10,9... | collective-permute-start | bytes 122888 | tf_op jit(solution)/shard_map/ppermute | solution.py:324
  40.8 0.8 collective-permute-start.8
  42.0 3.2 %collective-permute-done.8.refs_3_ = f32[80,128]{1,0:T(8,128)S(1)} collective-permute-done((f32[80,128]{1,0:T(8,128)S(1)}, f32[80,128]{1,0:T(8,128)S(1)}, u32[]{:S(2)}, u32[]{:S(2)}) %collective-permute-start.8) | collective-permute-done | bytes 40992 | tf_op jit(solution)/shard_map/ppermute | solution.py:324
  45.2 0.5 collective-permute-done.7.refs_2_
  45.7 0.7 coarse_mid.1
  46.4 19.6 %all_to_all.20.refs_0_ = f32[16,32,128]{2,1,0:T(8,128)S(1)} all-to-all(f32[16,32,128]{2,1,0:T(8,128)S(1)} %coarse_mid.1), channel_id=1, replica_groups=mesh['z'=8,'y'=4,'core'=2,'x'=4] {'core','z'}, dimensions={0} | all-to-all | bytes 524288 | tf_op jit(solution)/shard_map/all_to_all | solution.py:319
  65.9 3.2 %alpha.1 = (f32[32,32]{1,0:T(8,128)S(1)}, f32[32,32]{1,0:T(8,128)S(1)}, f32[16,16,128]{2,1,0:T(8,128)S(1)}) custom-call(f32[16,32,128]{2,1,0:T(8,128)S(1)} %all_to_all.20.refs_0_, f32[32,64]{1,0:T(8,128)S(1)} %get-tuple-element.25.refs_1_), custom_call_target="tpu_custom_call" | custom-call | flops 10000000 | bytes 409600 | tf_op jit(solution)/shard_map/alpha/pallas_call | solution.py:90
  69.2 12.3 %all_to_all.21.refs_1_ = f32[16,16,128]{2,1,0:T(8,128)S(1)} all-to-all(f32[16,16,128]{2,1,0:T(8,128)S(1)} %get-tuple-element.31), channel_id=1, replica_groups=mesh['z'=8,'y'=4,'core'=2,'x'=4] {'core','z'}, dimensions={0} | all-to-all | bytes 262144 | tf_op jit(solution)/shard_map/all_to_all | solution.py:319
  81.5 1.4 %coarse_sol.1 = f32[16,16,128]{2,1,0:T(8,128)} custom-call(f32[16,32,512]{2,1,0:T(8,128)S(1)} %all-to-all-done.refs_0_, f32[16,16,128]{2,1,0:T(8,128)S(1)} %all_to_all.21.refs_1_), custom_call_target="tpu_custom_call" | custom-call | flops 10000000 | bytes 1310720 | tf_op jit(solution)/shard_map/coarse_sol/pallas_call | solution.py:90
  82.9 4.0 %all-to-all-start.3 = ((f32[16,16,128]{2,1,0:T(8,128)}), f32[16,16,128]{2,1,0:T(8,128)S(1)}, u32[]{:S(2)}, u32[]{:S(2)}) async-start(f32[16,16,128]{2,1,0:T(8,128)} %coarse_sol.1), calls=%async_computation.3 | async-start | bytes 262144 | tf_op jit(solution)/shard_map/all_to_all | solution.py:319
  86.9 5.3 %updates.1 = (f32[1536,128]{1,0:T(8,128)}, f32[1536,128]{1,0:T(8,128)}, f32[32,6144]{1,0:T(8,128)S(1)}, f32[64,6144]{1,0:T(8,128)S(1)}) custom-call(f32[32,6144]{1,0:T(8,128)} %get-tuple-element.22.refs_0_, f32[1536,128]{1,0:T(8,128)} %bitcast.16, f32[128,128]{1,0:T(8,128)} %bitcast.19, f32[1536,128]{1,0:T(8,128)} %bitcast.17, f32[1536,128]{1,0:T(8,128)} %bitcast.11, ...), custom_call_target="tpu_custom_call" | custom-call | flops 75000000 | bytes 7933952 | tf_op jit(solution)/shard_map/updates/pallas_call | solution.py:90
  92.2 1.5 %all-to-all-done.3.refs_2_ = f32[16,16,128]{2,1,0:T(8,128)S(1)} async-done(((f32[16,16,128]{2,1,0:T(8,128)}), f32[16,16,128]{2,1,0:T(8,128)S(1)}, u32[]{:S(2)}, u32[]{:S(2)}) %all-to-all-start.3) | async-done | bytes 131104 | tf_op jit(solution)/shard_map/all_to_all | solution.py:319
  93.7 1.9 %new_direction.1 = f32[1536,128]{1,0:T(8,128)} custom-call(f32[64,6144]{1,0:T(8,128)S(1)} %get-tuple-element.29.refs_0_, f32[32,6144]{1,0:T(8,128)S(1)} %get-tuple-element.30.refs_1_, f32[16,16,128]{2,1,0:T(8,128)S(1)} %all-to-all-done.3.refs_2_, f32[32,32]{1,0:T(8,128)S(1)} %get-tuple-element.32.refs_3_), custom_call_target="tpu_custom_call" | custom-call | flops 25000000 | bytes 3280896 | tf_op jit(solution)/shard_map/new_direction/pallas_call | solution.py:90
  (10 shorter events, 0.7 us)
Async XLA Ops:
  3.9 18.4 %collective-permute-start = (f32[768,128]{1,0:T(8,128)}, f32[768,128]{1,0:T(8,128)S(1)}, u32[]{:S(2)}, u32[]{:S(2)}) collective-permute-start(f32[768,128]{1,0:T(8,128)} %get-tuple-element.18), channel_id=1, source_target_pairs={{0,4},{4,8},{8,12},{12,16},{16,20},{20,24},{24,28},{28,32},{32,36}... | collective-permute-start | bytes 1179656 | tf_op jit(solution)/shard_map/ppermute | solution.py:338
  8.5 13.8 %collective-permute-start.1 = (f32[768,128]{1,0:T(8,128)}, f32[768,128]{1,0:T(8,128)S(1)}, u32[]{:S(2)}, u32[]{:S(2)}) collective-permute-start(f32[768,128]{1,0:T(8,128)} %get-tuple-element.19), channel_id=1, source_target_pairs={{0,1},{1,2},{2,3},{4,5},{5,6},{6,7},{8,9},{9,10},{10,11},{12,13},{... | collective-permute-start | bytes 1179656 | tf_op jit(solution)/shard_map/ppermute | solution.py:341
  11.6 12.1 %collective-permute-start.2 = (f32[768,128]{1,0:T(8,128)S(1)}, f32[768,128]{1,0:T(8,128)S(1)}, u32[]{:S(2)}, u32[]{:S(2)}) collective-permute-start(f32[768,128]{1,0:T(8,128)S(1)} %get-tuple-element.20), channel_id=1, source_target_pairs={{1,0},{2,1},{3,2},{5,4},{6,5},{7,6},{9,8},{10,9},{11,10},{13,12},{... | collective-permute-start | bytes 1179656 | tf_op jit(solution)/shard_map/ppermute | solution.py:342
  12.9 10.9 %collective-permute-start.3 = (f32[768,128]{1,0:T(8,128)S(1)}, f32[768,128]{1,0:T(8,128)}, u32[]{:S(2)}, u32[]{:S(2)}) collective-permute-start(f32[768,128]{1,0:T(8,128)S(1)} %get-tuple-element.21), channel_id=1, source_target_pairs={{4,0},{8,4},{12,8},{16,12},{20,16},{24,20},{28,24},{32,28},{36,32}... | collective-permute-start | bytes 1179656 | tf_op jit(solution)/shard_map/ppermute | solution.py:339
  14.9 30.8 %all-to-all-start = ((f32[16,32,512]{2,1,0:T(8,128)}), f32[16,32,512]{2,1,0:T(8,128)S(1)}, u32[]{:S(2)}, u32[]{:S(2)}) async-start(f32[16,32,512]{2,1,0:T(8,128)} %get-tuple-element.23), calls=%async_computation | async-start | bytes 2097152 | tf_op jit(solution)/shard_map/all_to_all | solution.py:319
  29.3 4.2 %collective-permute-start.6 = (f32[32,128]{1,0:T(8,128)S(1)}, f32[32,128]{1,0:T(8,128)S(1)}, u32[]{:S(2)}, u32[]{:S(2)}) collective-permute-start(f32[32,128]{1,0:T(8,128)S(1)} %get-tuple-element.24.refs_0_), channel_id=1, source_target_pairs={{0,24},{8,0},{16,8},{24,16},{1,25},{9,1},{17,9},{25,17},{2,26},{10... | collective-permute-start | bytes 49160 | tf_op jit(solution)/shard_map/ppermute | solution.py:324
  32.6 4.1 %collective-permute-start.5 = (f32[32,128]{1,0:T(8,128)S(1)}, f32[32,128]{1,0:T(8,128)S(1)}, u32[]{:S(2)}, u32[]{:S(2)}) collective-permute-start(f32[32,128]{1,0:T(8,128)S(1)} %get-tuple-element.24.refs_0_), channel_id=1, source_target_pairs={{0,16},{8,24},{16,0},{24,8},{1,17},{9,25},{17,1},{25,9},{2,18},{10... | collective-permute-start | bytes 49160 | tf_op jit(solution)/shard_map/ppermute | solution.py:324
  32.7 4.1 %collective-permute-start.4 = (f32[32,128]{1,0:T(8,128)S(1)}, f32[32,128]{1,0:T(8,128)S(1)}, u32[]{:S(2)}, u32[]{:S(2)}) collective-permute-start(f32[32,128]{1,0:T(8,128)S(1)} %get-tuple-element.24.refs_0_), channel_id=1, source_target_pairs={{0,8},{8,16},{16,24},{24,0},{1,9},{9,17},{17,25},{25,1},{2,10},{10... | collective-permute-start | bytes 49160 | tf_op jit(solution)/shard_map/ppermute | solution.py:324
  36.9 5.1 %collective-permute-start.9 = (f32[80,128]{1,0:T(8,128)S(1)}, f32[80,128]{1,0:T(8,128)S(1)}, u32[]{:S(2)}, u32[]{:S(2)}) collective-permute-start(f32[80,128]{1,0:T(8,128)S(1)} %gather_y.1.refs_1_), channel_id=1, source_target_pairs={{0,3},{1,0},{2,1},{3,2},{4,7},{5,4},{6,5},{7,6},{8,11},{9,8},{10,9... | collective-permute-start | bytes 122888 | tf_op jit(solution)/shard_map/ppermute | solution.py:324
  40.8 4.4 %collective-permute-start.8 = (f32[80,128]{1,0:T(8,128)S(1)}, f32[80,128]{1,0:T(8,128)S(1)}, u32[]{:S(2)}, u32[]{:S(2)}) collective-permute-start(f32[80,128]{1,0:T(8,128)S(1)} %gather_y.1.refs_1_), channel_id=1, source_target_pairs={{0,2},{1,3},{2,0},{3,1},{4,6},{5,7},{6,4},{7,5},{8,10},{9,11},{10,... | collective-permute-start | bytes 122888 | tf_op jit(solution)/shard_map/ppermute | solution.py:324
  41.6 4.1 %collective-permute-start.7 = (f32[80,128]{1,0:T(8,128)S(1)}, f32[80,128]{1,0:T(8,128)S(1)}, u32[]{:S(2)}, u32[]{:S(2)}) collective-permute-start(f32[80,128]{1,0:T(8,128)S(1)} %gather_y.1.refs_1_), channel_id=1, source_target_pairs={{0,1},{1,2},{2,3},{3,0},{4,5},{5,6},{6,7},{7,4},{8,9},{9,10},{10,1... | collective-permute-start | bytes 122888 | tf_op jit(solution)/shard_map/ppermute | solution.py:324
  82.9 10.8 %all-to-all-start.3 = ((f32[16,16,128]{2,1,0:T(8,128)}), f32[16,16,128]{2,1,0:T(8,128)S(1)}, u32[]{:S(2)}, u32[]{:S(2)}) async-start(f32[16,16,128]{2,1,0:T(8,128)} %coarse_sol.1), calls=%async_computation.3 | async-start | bytes 262144 | tf_op jit(solution)/shard_map/all_to_all | solution.py:319

commit v5 on v4

--- a/solution.py
+++ b/solution.py
@@ -32,6 +32,9 @@
     def part(u, v):
         return lax.dot_general(u, v, (dims, ((), ())), preferred_element_type=jnp.float32)
 
+    if dims[0] == (1,) and a.shape[0] <= 512:
+        both = part(jnp.concatenate([a_high, a_low], axis=0), b_high)
+        return both[: a.shape[0]] + (part(a_high, b_low) + both[a.shape[0] :])
     return part(a_high, b_high) + (part(a_high, b_low) + part(a_low, b_high))
 
 
@@ -250,7 +253,7 @@
     total = jnp.sum(arrived[...], axis=0)
     mid_q, mid_r = total[:, :32], total[:, 32:64]
     gram, proj = total[:, 64:96], total[:, 96:]
-    base = inner[...] + dot(mid_q, total[:, : 2 * K], ((0,), (0,)))
+    base = inner[...] + dot3(mid_q, total[:, : 2 * K], ((0,), (0,)))
     row = lax.broadcasted_iota(jnp.int32, (K, K), 0)
     column = lax.broadcasted_iota(jnp.int32, (K, K), 1)
     work = jnp.concatenate([gram, (row == column).astype(jnp.float32), proj], axis=1)
@@ -268,7 +271,7 @@
     inverse = work[:, K : 2 * K]
     alpha[...] = mix
     gram_inverse[...] = inverse
-    after = dot(jnp.concatenate([mid_q, base[:, :K]], axis=0), mix)
+    after = dot3(jnp.concatenate([mid_q, base[:, :K]], axis=0), mix)
     coarse_mid = mid_r - after[:K]
     cross = base[:, K:] - after[K:]
     packed = packed4(coarse_mid, cross)

time: 97.2 us -> 97.1 us (level)
  no operation moved by 1% of the time
where the time goes in v5:
time: 97.1 us; the launch traced here: 95.6 us
  blocking collectives  31.9 us (33%)
  starting transfers between devices  31.7 us (33%)
  Pallas kernels  21.2 us (22%)
  waiting for transfers between devices  9.94 us (10%)
    all_to_all x2, blocking collectives, swapped(): return lax.all_to_all(array, axes, 0, 0, tiled=True)  31.9 us
    pallas_call x7, Pallas kernels, run(): pl.pallas_call(body, out_shape=[pltpu.HBM(o, jnp.float32) for o in outs[:...  18 us
    all_to_all x2, starting transfers between devices, swapped(): return lax.all_to_all(array, axes, 0, 0, tiled=True)  11.4 us
    ppermute x6, starting transfers between devices, from_all(): lax.ppermute(array, axis, [(i, (i + d) % n) for i in range(n)])  9.27 us
    ppermute x6, waiting for transfers between devices, from_all(): lax.ppermute(array, axis, [(i, (i + d) % n) for i in range(n)])  7 us
    ppermute x1, starting transfers between devices, on_device(): below_x = lax.ppermute(high_x, SUB, up_sub)  4.59 us
    pallas_call x1, Pallas kernels, halo_slabs(): pl.pallas_call(slab_kernel, out_shape=[jax.ShapeDtypeStruct((rows // 2, L...  3.23 us
    ppermute x1, starting transfers between devices, on_device(): below_y = lax.ppermute(high_y, 'x', up_inner)  3.14 us
  transfers between devices with their start and end apart: 12, of which 6 were waited for; matrix products, arithmetic and copies ran while one was open for 0% of the time, Pallas kernels for 11%

profile of v5, /device:TPU:1, one launch (start us, length us, event | category | flops | bytes accessed | tf_op | source)
XLA Modules:
  0.0 95.6 jit_solution(11174633761247404936)
XLA Ops:
  0.6 3.2 %halo_slabs.1 = (f32[768,128]{1,0:T(8,128)S(1)}, f32[768,128]{1,0:T(8,128)}, f32[768,128]{1,0:T(8,128)S(1)}, f32[768,128]{1,0:T(8,128)}, f32[16,32,512]{2,1,0:T(8,128)}) custom-call(f32[1536,128]{1,0:T(8,128)} %bitcast.9, f32[32,8192]{1,0:T(8,128)} %factor.1), custom_call_target="tpu_custom_call" | custom-call | flops 1000000 | bytes 5000000 | tf_op jit(solution)/shard_map/halo_slabs/pallas_call | solution.py:155
  3.9 4.6 %collective-permute-start = (f32[768,128]{1,0:T(8,128)}, f32[768,128]{1,0:T(8,128)S(1)}, u32[]{:S(2)}, u32[]{:S(2)}) collective-permute-start(f32[768,128]{1,0:T(8,128)} %get-tuple-element.18), channel_id=1, source_target_pairs={{0,4},{4,8},{8,12},{12,16},{16,20},{20,24},{24,28},{28,32},{32,36}... | collective-permute-start | bytes 1179656 | tf_op jit(solution)/shard_map/ppermute | solution.py:341
  8.5 3.1 %collective-permute-start.1 = (f32[768,128]{1,0:T(8,128)}, f32[768,128]{1,0:T(8,128)S(1)}, u32[]{:S(2)}, u32[]{:S(2)}) collective-permute-start(f32[768,128]{1,0:T(8,128)} %get-tuple-element.19), channel_id=1, source_target_pairs={{0,1},{1,2},{2,3},{4,5},{5,6},{6,7},{8,9},{9,10},{10,11},{12,13},{... | collective-permute-start | bytes 1179656 | tf_op jit(solution)/shard_map/ppermute | solution.py:344
  11.6 1.3 %collective-permute-start.2 = (f32[768,128]{1,0:T(8,128)S(1)}, f32[768,128]{1,0:T(8,128)S(1)}, u32[]{:S(2)}, u32[]{:S(2)}) collective-permute-start(f32[768,128]{1,0:T(8,128)S(1)} %get-tuple-element.20), channel_id=1, source_target_pairs={{1,0},{2,1},{3,2},{5,4},{6,5},{7,6},{9,8},{10,9},{11,10},{13,12},{... | collective-permute-start | bytes 1179656 | tf_op jit(solution)/shard_map/ppermute | solution.py:345
  12.9 1.9 %collective-permute-start.3 = (f32[768,128]{1,0:T(8,128)S(1)}, f32[768,128]{1,0:T(8,128)}, u32[]{:S(2)}, u32[]{:S(2)}) collective-permute-start(f32[768,128]{1,0:T(8,128)S(1)} %get-tuple-element.21), channel_id=1, source_target_pairs={{4,0},{8,4},{12,8},{16,12},{20,16},{24,20},{28,24},{32,28},{36,32}... | collective-permute-start | bytes 1179656 | tf_op jit(solution)/shard_map/ppermute | solution.py:342
  14.9 7.4 %all-to-all-start = ((f32[16,32,512]{2,1,0:T(8,128)}), f32[16,32,512]{2,1,0:T(8,128)S(1)}, u32[]{:S(2)}, u32[]{:S(2)}) async-start(f32[16,32,512]{2,1,0:T(8,128)} %get-tuple-element.23), calls=%async_computation | async-start | bytes 2097152 | tf_op jit(solution)/shard_map/all_to_all | solution.py:322
  22.3 1.5 %collective-permute-done.2.refs_7_ = f32[768,128]{1,0:T(8,128)S(1)} collective-permute-done((f32[768,128]{1,0:T(8,128)S(1)}, f32[768,128]{1,0:T(8,128)S(1)}, u32[]{:S(2)}, u32[]{:S(2)}) %collective-permute-start.2) | collective-permute-done | bytes 393248 | tf_op jit(solution)/shard_map/ppermute | solution.py:345
  23.8 5.5 %image.1 = (f32[32,6144]{1,0:T(8,128)}, f32[32,128]{1,0:T(8,128)S(1)}, f32[32,64]{1,0:T(8,128)S(1)}) custom-call(f32[1536,128]{1,0:T(8,128)} %bitcast.10, f32[16,128]{1,0:T(8,128)} %bitcast.22, f32[128,128]{1,0:T(8,128)} %bitcast.18, f32[1536,128]{1,0:T(8,128)} %bitcast.13, f32[1536,128]{1,0:T(8,128)} %bitcast.15, ...), custom_call_target="tpu_custom_call" | custom-call | flops 49999998976 | bytes 4816896 | tf_op jit(solution)/shard_map/image/pallas_call | solution.py:93
  29.3 3.4 %collective-permute-start.6 = (f32[32,128]{1,0:T(8,128)S(1)}, f32[32,128]{1,0:T(8,128)S(1)}, u32[]{:S(2)}, u32[]{:S(2)}) collective-permute-start(f32[32,128]{1,0:T(8,128)S(1)} %get-tuple-element.24.refs_0_), channel_id=1, source_target_pairs={{0,24},{8,0},{16,8},{24,16},{1,25},{9,1},{17,9},{25,17},{2,26},{10... | collective-permute-start | bytes 49160 | tf_op jit(solution)/shard_map/ppermute | solution.py:327
  32.7 0.8 collective-permute-start.4
  33.5 3.2 %collective-permute-done.5.refs_2_ = f32[32,128]{1,0:T(8,128)S(1)} collective-permute-done((f32[32,128]{1,0:T(8,128)S(1)}, f32[32,128]{1,0:T(8,128)S(1)}, u32[]{:S(2)}, u32[]{:S(2)}) %collective-permute-start.5) | collective-permute-done | bytes 16416 | tf_op jit(solution)/shard_map/ppermute | solution.py:327
  36.9 4.0 %collective-permute-start.9 = (f32[80,128]{1,0:T(8,128)S(1)}, f32[80,128]{1,0:T(8,128)S(1)}, u32[]{:S(2)}, u32[]{:S(2)}) collective-permute-start(f32[80,128]{1,0:T(8,128)S(1)} %gather_y.1.refs_1_), channel_id=1, source_target_pairs={{0,3},{1,0},{2,1},{3,2},{4,7},{5,4},{6,5},{7,6},{8,11},{9,8},{10,9... | collective-permute-start | bytes 122888 | tf_op jit(solution)/shard_map/ppermute | solution.py:327
  40.8 0.8 collective-permute-start.8
  42.0 3.2 %collective-permute-done.8.refs_3_ = f32[80,128]{1,0:T(8,128)S(1)} collective-permute-done((f32[80,128]{1,0:T(8,128)S(1)}, f32[80,128]{1,0:T(8,128)S(1)}, u32[]{:S(2)}, u32[]{:S(2)}) %collective-permute-start.8) | collective-permute-done | bytes 40992 | tf_op jit(solution)/shard_map/ppermute | solution.py:327
  45.2 0.5 collective-permute-done.7.refs_2_
  45.7 0.6 coarse_mid.1
  46.3 19.6 %all_to_all.20.refs_0_ = f32[16,32,128]{2,1,0:T(8,128)S(1)} all-to-all(f32[16,32,128]{2,1,0:T(8,128)S(1)} %coarse_mid.1), channel_id=1, replica_groups=mesh['z'=8,'y'=4,'core'=2,'x'=4] {'core','z'}, dimensions={0} | all-to-all | bytes 524288 | tf_op jit(solution)/shard_map/all_to_all | solution.py:322
  65.8 3.2 %alpha.1 = (f32[32,32]{1,0:T(8,128)S(1)}, f32[32,32]{1,0:T(8,128)S(1)}, f32[16,16,128]{2,1,0:T(8,128)S(1)}) custom-call(f32[16,32,128]{2,1,0:T(8,128)S(1)} %all_to_all.20.refs_0_, f32[32,64]{1,0:T(8,128)S(1)} %get-tuple-element.25.refs_1_), custom_call_target="tpu_custom_call" | custom-call | flops 10000000 | bytes 409600 | tf_op jit(solution)/shard_map/alpha/pallas_call | solution.py:93
  69.0 12.3 %all_to_all.21.refs_1_ = f32[16,16,128]{2,1,0:T(8,128)S(1)} all-to-all(f32[16,16,128]{2,1,0:T(8,128)S(1)} %get-tuple-element.31), channel_id=1, replica_groups=mesh['z'=8,'y'=4,'core'=2,'x'=4] {'core','z'}, dimensions={0} | all-to-all | bytes 262144 | tf_op jit(solution)/shard_map/all_to_all | solution.py:322
  81.4 1.4 %coarse_sol.1 = f32[16,16,128]{2,1,0:T(8,128)} custom-call(f32[16,32,512]{2,1,0:T(8,128)S(1)} %all-to-all-done.refs_0_, f32[16,16,128]{2,1,0:T(8,128)S(1)} %all_to_all.21.refs_1_), custom_call_target="tpu_custom_call" | custom-call | flops 10000000 | bytes 1310720 | tf_op jit(solution)/shard_map/coarse_sol/pallas_call | solution.py:93
  82.7 4.0 %all-to-all-start.3 = ((f32[16,16,128]{2,1,0:T(8,128)}), f32[16,16,128]{2,1,0:T(8,128)S(1)}, u32[]{:S(2)}, u32[]{:S(2)}) async-start(f32[16,16,128]{2,1,0:T(8,128)} %coarse_sol.1), calls=%async_computation.3 | async-start | bytes 262144 | tf_op jit(solution)/shard_map/all_to_all | solution.py:322
  86.7 5.4 %updates.1 = (f32[1536,128]{1,0:T(8,128)}, f32[1536,128]{1,0:T(8,128)}, f32[32,6144]{1,0:T(8,128)S(1)}, f32[64,6144]{1,0:T(8,128)S(1)}) custom-call(f32[32,6144]{1,0:T(8,128)} %get-tuple-element.22.refs_0_, f32[1536,128]{1,0:T(8,128)} %bitcast.16, f32[128,128]{1,0:T(8,128)} %bitcast.19, f32[1536,128]{1,0:T(8,128)} %bitcast.17, f32[1536,128]{1,0:T(8,128)} %bitcast.11, ...), custom_call_target="tpu_custom_call" | custom-call | flops 75000000 | bytes 7933952 | tf_op jit(solution)/shard_map/updates/pallas_call | solution.py:93
  92.1 1.5 %all-to-all-done.3.refs_2_ = f32[16,16,128]{2,1,0:T(8,128)S(1)} async-done(((f32[16,16,128]{2,1,0:T(8,128)}), f32[16,16,128]{2,1,0:T(8,128)S(1)}, u32[]{:S(2)}, u32[]{:S(2)}) %all-to-all-start.3) | async-done | bytes 131104 | tf_op jit(solution)/shard_map/all_to_all | solution.py:322
  93.6 1.9 %new_direction.1 = f32[1536,128]{1,0:T(8,128)} custom-call(f32[64,6144]{1,0:T(8,128)S(1)} %get-tuple-element.29.refs_0_, f32[32,6144]{1,0:T(8,128)S(1)} %get-tuple-element.30.refs_1_, f32[16,16,128]{2,1,0:T(8,128)S(1)} %all-to-all-done.3.refs_2_, f32[32,32]{1,0:T(8,128)S(1)} %get-tuple-element.32.refs_3_), custom_call_target="tpu_custom_call" | custom-call | flops 25000000 | bytes 3280896 | tf_op jit(solution)/shard_map/new_direction/pallas_call | solution.py:93
  (10 shorter events, 0.6 us)
Async XLA Ops:
  3.9 18.4 %collective-permute-start = (f32[768,128]{1,0:T(8,128)}, f32[768,128]{1,0:T(8,128)S(1)}, u32[]{:S(2)}, u32[]{:S(2)}) collective-permute-start(f32[768,128]{1,0:T(8,128)} %get-tuple-element.18), channel_id=1, source_target_pairs={{0,4},{4,8},{8,12},{12,16},{16,20},{20,24},{24,28},{28,32},{32,36}... | collective-permute-start | bytes 1179656 | tf_op jit(solution)/shard_map/ppermute | solution.py:341
  8.5 13.8 %collective-permute-start.1 = (f32[768,128]{1,0:T(8,128)}, f32[768,128]{1,0:T(8,128)S(1)}, u32[]{:S(2)}, u32[]{:S(2)}) collective-permute-start(f32[768,128]{1,0:T(8,128)} %get-tuple-element.19), channel_id=1, source_target_pairs={{0,1},{1,2},{2,3},{4,5},{5,6},{6,7},{8,9},{9,10},{10,11},{12,13},{... | collective-permute-start | bytes 1179656 | tf_op jit(solution)/shard_map/ppermute | solution.py:344
  11.6 12.1 %collective-permute-start.2 = (f32[768,128]{1,0:T(8,128)S(1)}, f32[768,128]{1,0:T(8,128)S(1)}, u32[]{:S(2)}, u32[]{:S(2)}) collective-permute-start(f32[768,128]{1,0:T(8,128)S(1)} %get-tuple-element.20), channel_id=1, source_target_pairs={{1,0},{2,1},{3,2},{5,4},{6,5},{7,6},{9,8},{10,9},{11,10},{13,12},{... | collective-permute-start | bytes 1179656 | tf_op jit(solution)/shard_map/ppermute | solution.py:345
  12.9 10.9 %collective-permute-start.3 = (f32[768,128]{1,0:T(8,128)S(1)}, f32[768,128]{1,0:T(8,128)}, u32[]{:S(2)}, u32[]{:S(2)}) collective-permute-start(f32[768,128]{1,0:T(8,128)S(1)} %get-tuple-element.21), channel_id=1, source_target_pairs={{4,0},{8,4},{12,8},{16,12},{20,16},{24,20},{28,24},{32,28},{36,32}... | collective-permute-start | bytes 1179656 | tf_op jit(solution)/shard_map/ppermute | solution.py:342
  14.9 30.8 %all-to-all-start = ((f32[16,32,512]{2,1,0:T(8,128)}), f32[16,32,512]{2,1,0:T(8,128)S(1)}, u32[]{:S(2)}, u32[]{:S(2)}) async-start(f32[16,32,512]{2,1,0:T(8,128)} %get-tuple-element.23), calls=%async_computation | async-start | bytes 2097152 | tf_op jit(solution)/shard_map/all_to_all | solution.py:322
  29.3 4.2 %collective-permute-start.6 = (f32[32,128]{1,0:T(8,128)S(1)}, f32[32,128]{1,0:T(8,128)S(1)}, u32[]{:S(2)}, u32[]{:S(2)}) collective-permute-start(f32[32,128]{1,0:T(8,128)S(1)} %get-tuple-element.24.refs_0_), channel_id=1, source_target_pairs={{0,24},{8,0},{16,8},{24,16},{1,25},{9,1},{17,9},{25,17},{2,26},{10... | collective-permute-start | bytes 49160 | tf_op jit(solution)/shard_map/ppermute | solution.py:327
  32.6 4.1 %collective-permute-start.5 = (f32[32,128]{1,0:T(8,128)S(1)}, f32[32,128]{1,0:T(8,128)S(1)}, u32[]{:S(2)}, u32[]{:S(2)}) collective-permute-start(f32[32,128]{1,0:T(8,128)S(1)} %get-tuple-element.24.refs_0_), channel_id=1, source_target_pairs={{0,16},{8,24},{16,0},{24,8},{1,17},{9,25},{17,1},{25,9},{2,18},{10... | collective-permute-start | bytes 49160 | tf_op jit(solution)/shard_map/ppermute | solution.py:327
  32.7 4.1 %collective-permute-start.4 = (f32[32,128]{1,0:T(8,128)S(1)}, f32[32,128]{1,0:T(8,128)S(1)}, u32[]{:S(2)}, u32[]{:S(2)}) collective-permute-start(f32[32,128]{1,0:T(8,128)S(1)} %get-tuple-element.24.refs_0_), channel_id=1, source_target_pairs={{0,8},{8,16},{16,24},{24,0},{1,9},{9,17},{17,25},{25,1},{2,10},{10... | collective-permute-start | bytes 49160 | tf_op jit(solution)/shard_map/ppermute | solution.py:327
  36.9 5.1 %collective-permute-start.9 = (f32[80,128]{1,0:T(8,128)S(1)}, f32[80,128]{1,0:T(8,128)S(1)}, u32[]{:S(2)}, u32[]{:S(2)}) collective-permute-start(f32[80,128]{1,0:T(8,128)S(1)} %gather_y.1.refs_1_), channel_id=1, source_target_pairs={{0,3},{1,0},{2,1},{3,2},{4,7},{5,4},{6,5},{7,6},{8,11},{9,8},{10,9... | collective-permute-start | bytes 122888 | tf_op jit(solution)/shard_map/ppermute | solution.py:327
  40.8 4.4 %collective-permute-start.8 = (f32[80,128]{1,0:T(8,128)S(1)}, f32[80,128]{1,0:T(8,128)S(1)}, u32[]{:S(2)}, u32[]{:S(2)}) collective-permute-start(f32[80,128]{1,0:T(8,128)S(1)} %gather_y.1.refs_1_), channel_id=1, source_target_pairs={{0,2},{1,3},{2,0},{3,1},{4,6},{5,7},{6,4},{7,5},{8,10},{9,11},{10,... | collective-permute-start | bytes 122888 | tf_op jit(solution)/shard_map/ppermute | solution.py:327
  41.6 4.1 %collective-permute-start.7 = (f32[80,128]{1,0:T(8,128)S(1)}, f32[80,128]{1,0:T(8,128)S(1)}, u32[]{:S(2)}, u32[]{:S(2)}) collective-permute-start(f32[80,128]{1,0:T(8,128)S(1)} %gather_y.1.refs_1_), channel_id=1, source_target_pairs={{0,1},{1,2},{2,3},{3,0},{4,5},{5,6},{6,7},{7,4},{8,9},{9,10},{10,1... | collective-permute-start | bytes 122888 | tf_op jit(solution)/shard_map/ppermute | solution.py:327
  82.7 10.8 %all-to-all-start.3 = ((f32[16,16,128]{2,1,0:T(8,128)}), f32[16,16,128]{2,1,0:T(8,128)S(1)}, u32[]{:S(2)}, u32[]{:S(2)}) async-start(f32[16,16,128]{2,1,0:T(8,128)} %coarse_sol.1), calls=%async_computation.3 | async-start | bytes 262144 | tf_op jit(solution)/shard_map/all_to_all | solution.py:322
